TPU v7x, 512 devices: a whole 4x4x16 slice. The times are simulated.
512 devices in a mesh: slab: 32 (over z_hi, y, x), patch: 16 (over z_lo, core).
Axes of the slice: x: 4, y: 4, z: 16 (z_hi: 2, z_lo: 8; z = z_hi * 8 + z_lo), core: 2. Of those that a mesh axis runs over, the one named last changes fastest.
Arguments:
- rhs: float32 [32, 16, 128, 2, 256], P('slab', 'patch'), may hold values from -12 to 12
- face_blocks: bfloat16 [32, 16, 4, 256, 256], P('slab', 'patch'), may hold values from -1 to 4, as said below
- interior_inverse: bfloat16 [32, 16, 1024, 1024], P('slab', 'patch'), may hold values from -1 to 1, as said below
- coarse_inverse: bfloat16 [8192, 8192], P('slab', 'patch'), may hold values from -1 to 3, as said below
- primal_ids: int32 [32, 16, 16], P('slab', 'patch'), may hold values from 0 to 1023, as said below
Outputs:
- solution: float32 [32, 16, 128, 2, 256], P('slab', 'patch')
- residual: float32 [32, 16, 128, 2, 256], P('slab', 'patch')
Inputs may be any that keep to these rules, and one draw needn't show every extreme that they name: `face_blocks`: each block is symmetric positive definite. `interior_inverse`: each patch's matrix is symmetric. `coarse_inverse`: the matrix, read with columns in mesh order of patches, is symmetric positive definite. `primal_ids`: each patch's 16 entries are distinct.
All inputs are finite; a program needn't handle non-finite values.
Results may differ from a plain program's by a relative error of at most 0.0095.
The roundings to bfloat16 on the way count: a program that leaves them out, or rounds other values in their place, can miss the bound.
Values may be sent and summed in bfloat16 or wider, within the bound.
No kernel may reach another device: no remote copies, remote signals or barrier semaphores. Data moves between devices by JAX's collectives and lax.ppermute only.
A program may use at most 64 MiB of HBM per device.

v0:
```python
import jax
import jax.numpy as jnp
from jax import lax
from jax.sharding import PartitionSpec as P

F = 256
NI = 1024
RHS = 128
ITERS = 2


def from_behind(value, axis, by):
    count = lax.axis_size(axis)
    return lax.ppermute(value, axis, [(i, (i + by) % count) for i in range(count)])


def face_solve(factors, vector):
    moved = jnp.moveaxis(vector, -3, -1)
    middle = jax.scipy.linalg.solve_triangular(factors, moved, lower=True)
    result = jax.scipy.linalg.solve_triangular(factors, middle, lower=True, trans=1)
    return jnp.moveaxis(result, -1, -3)


def face_apply(blocks, vb):
    return jnp.einsum("fij,rfj->rfi", blocks, vb, preferred_element_type=jnp.float32)


def interior_apply(inverse, vb):
    flat = vb.reshape(vb.shape[0], -1)
    product = lax.dot_general(
        flat, inverse, (((1,), (1,)), ((), ())), preferred_element_type=jnp.float32
    )
    return product.reshape(vb.shape)


def view_rounded(owned_field):
    rounded = owned_field.astype(jnp.bfloat16)
    from_slab = from_behind(rounded[:, 0], "slab", 1)
    from_patch = from_behind(rounded[:, 1], "patch", 1)
    return jnp.stack([rounded[:, 0], rounded[:, 1], from_slab, from_patch], axis=1)


def assemble(patch_terms):
    to_slab = from_behind(patch_terms[:, 2], "slab", -1)
    to_patch = from_behind(patch_terms[:, 3], "patch", -1)
    return jnp.stack([patch_terms[:, 0] + to_slab, patch_terms[:, 1] + to_patch], axis=1)


def inner_local(first, second):
    return jnp.sum(first * second, axis=(1, 2))


def on_device(rhs, face_blocks, interior_inverse, coarse_inverse, primal_ids):
    right_side = rhs[0, 0]
    blocks = face_blocks[0, 0]
    inverse = interior_inverse[0, 0]
    indices = primal_ids[0, 0]
    back_slab_block = from_behind(blocks[2], "slab", -1)
    back_patch_block = from_behind(blocks[3], "patch", -1)
    face_sums = [
        blocks[0].astype(jnp.float32) + back_slab_block.astype(jnp.float32),
        blocks[1].astype(jnp.float32) + back_patch_block.astype(jnp.float32),
    ]
    onehot = (indices[:, None] == lax.iota(jnp.int32, NI)[None, :]).astype(jnp.bfloat16)

    def coarse_term(hb):
        product = face_apply(blocks, hb).reshape(RHS, NI)
        coarse_rhs = jnp.take(product, indices, axis=1).T.astype(jnp.bfloat16)
        gathered = lax.all_gather(coarse_rhs, "slab", axis=0, tiled=True)
        coarse_sol = lax.psum_scatter(
            jnp.dot(coarse_inverse, gathered, preferred_element_type=jnp.float32),
            "patch",
            scatter_dimension=0,
            tiled=True,
        ).astype(jnp.bfloat16)
        spread = lax.dot_general(
            coarse_sol, onehot, (((0,), (0,)), ((), ())), preferred_element_type=jnp.float32
        )
        spread = spread.astype(jnp.bfloat16).reshape(RHS, 4, F)
        return interior_apply(inverse, hb) + face_apply(blocks, spread)

    factors = jnp.linalg.cholesky(jnp.stack(face_sums))

    def apply_m(vector):
        lifted = face_solve(factors, vector)
        return lifted + face_solve(factors, assemble(coarse_term(view_rounded(lifted))))

    def total_sum(value):
        return lax.psum(value, ("slab", "patch"))

    solution = jnp.zeros_like(right_side)
    residual = right_side
    direction = apply_m(residual)
    rz_now = total_sum(inner_local(residual, direction))
    for iteration in range(ITERS):
        vb = view_rounded(direction)
        mapped = assemble(face_apply(blocks, vb) - interior_apply(inverse, vb))
        step_size = rz_now / total_sum(inner_local(direction, mapped))
        solution = solution + step_size[:, None, None] * direction
        residual = residual - step_size[:, None, None] * mapped
        if iteration + 1 < ITERS:
            precond = apply_m(residual)
            rz_next = total_sum(inner_local(residual, precond))
            direction = precond + (rz_next / rz_now)[:, None, None] * direction
            rz_now = rz_next
    return (solution[None, None], residual[None, None])


def solution(mesh):
    return jax.shard_map(
        on_device,
        mesh=mesh,
        in_specs=(
            P("slab", "patch", None, None, None),
            P("slab", "patch", None, None, None),
            P("slab", "patch", None, None),
            P("slab", "patch"),
            P("slab", "patch", None),
        ),
        out_specs=(P("slab", "patch", None, None, None), P("slab", "patch", None, None, None)),
        check_vma=False,
    )
```

profile of v0, /device:TPU:1, one launch (start us, length us, event | category | flops | bytes accessed | tf_op | source)
XLA Modules:
  0.0 1184.2 jit_solution(8006487325135948689)
XLA Ops:
  8.6 8.8 collective-permute-start.1
  17.5 14.7 %collective-permute-start = (bf16[256,256]{0,1:T(8,128)(2,1)S(1)}, bf16[256,256]{0,1:T(8,128)(2,1)S(1)}, u32[]{:S(2)}, u32[]{:S(2)}) collective-permute-start(bf16[256,256]{0,1:T(8,128)(2,1)S(1)} %bitcast.381), channel_id=1, source_target_pairs={{0,496},{16,0},{32,16},{48,32},{64,48},{80,64},{96,80},{112,96},{1... | collective-permute-start | bytes 393224 | tf_op jit(solution)/shard_map/ppermute | solution.py:14
  35.7 7.3 collective-permute-done
  46.0 23.5 %custom-call.19 = f32[2,128,128]{2,1,0:T(8,128)S(1)} custom-call(f32[2,128,128]{2,1,0:T(8,128)S(1)} %cholesky.122), custom_call_target="Cholesky" | custom-call | tf_op jit(solution)/shard_map/jit(cholesky)/cholesky | solution.py:82
  69.5 19.7 %custom-call.20 = f32[2,1,128,128]{2,3,1,0:T(8,128)S(1)} custom-call(f32[2,1,128,128]{3,2,1,0:T(8,128)S(1)} %select_bitcast_fusion), custom_call_target="InvertDiagBlocksLowerTriangular" | custom-call | tf_op jit(solution)/shard_map/jit(cholesky)/cholesky | solution.py:82
  91.7 23.5 %custom-call.21 = f32[2,128,128]{2,1,0:T(8,128)S(1)} custom-call(f32[2,128,128]{2,1,0:T(8,128)S(1)} %convolution_subtract_fusion.8), custom_call_target="Cholesky" | custom-call | tf_op jit(solution)/shard_map/jit(cholesky)/cholesky | solution.py:82
  115.6 5.1 while.16
  120.7 40.1 %custom-call.29 = f32[2,2,128,128]{2,3,1,0:T(8,128)S(1)} custom-call(f32[2,2,128,128]{3,2,1,0:T(8,128)} %bitcast.393), custom_call_target="InvertDiagBlocksLowerTriangular" | custom-call | tf_op jit(solution)/shard_map/jit(_solve_triangular)/vmap()/triangular_solve | solution.py:20
  167.3 3.9 collective-permute-start.3
  171.2 13.3 %collective-permute-done.2 = bf16[128,256]{0,1:T(8,128)(2,1)S(1)} collective-permute-done((bf16[128,256]{0,1:T(8,128)(2,1)S(1)}, bf16[128,256]{0,1:T(8,128)(2,1)S(1)}, u32[]{:S(2)}, u32[]{:S(2)}) %collective-permute-start.2) | collective-permute-done | bytes 65568 | tf_op jit(solution)/shard_map/ppermute | solution.py:14
  189.5 134.8 %all_gather.6 = bf16[512,128]{1,0:T(8,128)(2,1)S(1)} all-gather(bf16[16,128]{1,0:T(8,128)(2,1)S(1)} %fusion.82), channel_id=1, replica_groups=mesh['slab'=32,'patch'=16] {'slab'}, dimensions={0}, use_global_device_ids=true | all-gather | bytes 135168 | tf_op jit(solution)/shard_map/all_gather | solution.py:69
  329.6 107.4 %reduce-scatter.7.cloned.1.call-done = f32[16,128]{1,0:T(8,128)} async-done(((f32[256,128]{1,0:T(8,128)}), f32[16,128]{1,0:T(8,128)}) %reduce-scatter.7.cloned.1.call-update) | async-done | bytes 8208
  441.6 15.8 %collective-permute-start.4 = (f32[128,256]{1,0:T(8,128)S(1)}, f32[128,256]{1,0:T(8,128)S(1)}, u32[]{:S(2)}, u32[]{:S(2)}) collective-permute-start(f32[128,256]{1,0:T(8,128)S(1)} %get-tuple-element.115), channel_id=1, source_target_pairs={{0,496},{16,0},{32,16},{48,32},{64,48},{80,64},{96,80},{112,96},{1... | collective-permute-start | bytes 393224 | tf_op jit(solution)/shard_map/ppermute | solution.py:14
  457.4 3.8 collective-permute-start.5
  461.3 2.9 collective-permute-done.5
  470.3 14.9 %collective-permute-done.6 = bf16[128,256]{0,1:T(8,128)(2,1)S(1)} collective-permute-done((bf16[128,256]{0,1:T(8,128)(2,1)S(1)}, bf16[128,256]{0,1:T(8,128)(2,1)S(1)}, u32[]{:S(2)}, u32[]{:S(2)}) %collective-permute-start.6) | collective-permute-done | bytes 65568 | tf_op jit(solution)/shard_map/ppermute | solution.py:14
  486.3 9.1 collective-permute-start.8
  495.4 11.9 %collective-permute-start.9 = (f32[128,256]{0,1:T(8,128)S(1)}, f32[128,256]{0,1:T(8,128)S(1)}, u32[]{:S(2)}, u32[]{:S(2)}) collective-permute-start(f32[128,256]{0,1:T(8,128)S(1)} %get-tuple-element.112), channel_id=1, source_target_pairs={{0,15},{1,0},{2,1},{3,2},{4,3},{5,4},{6,5},{7,6},{8,7},{9,8},{10,9... | collective-permute-start | bytes 393224 | tf_op jit(solution)/shard_map/ppermute | solution.py:14
  509.7 102.3 %all-reduce.1 = (f32[128]{0:T(128)}, f32[128]{0:T(128)}) all-reduce(f32[128]{0:T(128)S(1)} %get-tuple-element.74, f32[128]{0:T(128)S(1)} %get-tuple-element.73), channel_id=1, replica_groups=mesh['slab'=32,'patch'=16] {'slab','patch'}, use_global_device_ids=true, to_apply=%region_6.10 | all-reduce | flops 256 | bytes 2048 | tf_op jit(solution)/shard_map/psum | solution.py:89
  618.3 4.1 collective-permute-start.11
  622.4 12.1 %collective-permute-done.10 = bf16[128,256]{0,1:T(8,128)(2,1)S(1)} collective-permute-done((bf16[128,256]{0,1:T(8,128)(2,1)S(1)}, bf16[128,256]{0,1:T(8,128)(2,1)S(1)}, u32[]{:S(2)}, u32[]{:S(2)}) %collective-permute-start.10) | collective-permute-done | bytes 65568 | tf_op jit(solution)/shard_map/ppermute | solution.py:14
  640.3 135.3 %all_gather.7 = bf16[512,128]{1,0:T(8,128)(2,1)S(1)} all-gather(bf16[16,128]{1,0:T(8,128)(2,1)S(1)} %fusion.83), channel_id=1, replica_groups=mesh['slab'=32,'patch'=16] {'slab'}, dimensions={0}, use_global_device_ids=true | all-gather | bytes 135168 | tf_op jit(solution)/shard_map/all_gather | solution.py:69
  780.8 109.2 %reduce-scatter.9.cloned.1.call-done = f32[16,128]{1,0:T(8,128)} async-done(((f32[256,128]{1,0:T(8,128)}), f32[16,128]{1,0:T(8,128)}) %reduce-scatter.9.cloned.1.call-update) | async-done | bytes 8208
  894.6 15.9 %collective-permute-start.12 = (f32[128,256]{1,0:T(8,128)S(1)}, f32[128,256]{1,0:T(8,128)S(1)}, u32[]{:S(2)}, u32[]{:S(2)}) collective-permute-start(f32[128,256]{1,0:T(8,128)S(1)} %get-tuple-element.109), channel_id=1, source_target_pairs={{0,496},{16,0},{32,16},{48,32},{64,48},{80,64},{96,80},{112,96},{1... | collective-permute-start | bytes 393224 | tf_op jit(solution)/shard_map/ppermute | solution.py:14
  910.6 3.9 collective-permute-start.13
  914.5 2.9 collective-permute-done.13
  919.7 107.2 %psum.30 = f32[128]{0:T(128)S(1)} all-reduce(f32[128]{0:T(128)S(1)} %get-tuple-element.87), channel_id=1, replica_groups=mesh['slab'=32,'patch'=16] {'slab','patch'}, use_global_device_ids=true, to_apply=%region_11.15 | all-reduce | flops 128 | bytes 1024 | tf_op jit(solution)/shard_map/psum | solution.py:89
  1029.9 2.7 collective-permute-start.15
  1032.6 13.4 %collective-permute-done.14 = bf16[128,256]{0,1:T(8,128)(2,1)S(1)} collective-permute-done((bf16[128,256]{0,1:T(8,128)(2,1)S(1)}, bf16[128,256]{0,1:T(8,128)(2,1)S(1)}, u32[]{:S(2)}, u32[]{:S(2)}) %collective-permute-start.14) | collective-permute-done | bytes 65568 | tf_op jit(solution)/shard_map/ppermute | solution.py:14
  1047.1 4.9 collective-permute-start.16
  1052.0 11.9 %collective-permute-start.17 = (f32[128,256]{0,1:T(8,128)S(1)}, f32[128,256]{0,1:T(8,128)S(1)}, u32[]{:S(2)}, u32[]{:S(2)}) collective-permute-start(f32[128,256]{0,1:T(8,128)S(1)} %get-tuple-element.106), channel_id=1, source_target_pairs={{0,15},{1,0},{2,1},{3,2},{4,3},{5,4},{6,5},{7,6},{8,7},{9,8},{10,9... | collective-permute-start | bytes 393224 | tf_op jit(solution)/shard_map/ppermute | solution.py:14
  1066.0 108.7 %psum.31 = f32[128]{0:T(128)S(1)} all-reduce(f32[128]{0:T(128)S(1)} %fusion.15), channel_id=1, replica_groups=mesh['slab'=32,'patch'=16] {'slab','patch'}, use_global_device_ids=true, to_apply=%region_13.17 | all-reduce | flops 128 | bytes 1024 | tf_op jit(solution)/shard_map/psum | solution.py:89
  (190 shorter events, 79.5 us)
Async XLA Ops:
  7.2 432.6 %copy-start = (bf16[1,1,1024,1024]{3,2,1,0:T(8,128)(2,1)S(1)}, bf16[1,1,1024,1024]{3,2,1,0:T(8,128)(2,1)}, u32[]{:S(2)}) copy-start(bf16[1,1,1024,1024]{3,2,1,0:T(8,128)(2,1)} %param.13) | copy-start | bytes 6291460
  7.2 429.8 %reduce-scatter.7.cloned.1.call-start = ((), (), s32[]{:S(2)}) async-start(), calls=%async_computation.2 | async-start | bytes 139264
  8.6 27.0 %collective-permute-start.1 = (bf16[256,256]{0,1:T(8,128)(2,1)S(1)}, bf16[256,256]{0,1:T(8,128)(2,1)S(1)}, u32[]{:S(2)}, u32[]{:S(2)}) collective-permute-start(bf16[256,256]{0,1:T(8,128)(2,1)S(1)} %bitcast.382), channel_id=1, source_target_pairs={{0,15},{1,0},{2,1},{3,2},{4,3},{5,4},{6,5},{7,6},{8,7},{9,8},{10,9... | collective-permute-start | bytes 393224 | tf_op jit(solution)/shard_map/ppermute | solution.py:14
  17.5 25.5 %collective-permute-start = (bf16[256,256]{0,1:T(8,128)(2,1)S(1)}, bf16[256,256]{0,1:T(8,128)(2,1)S(1)}, u32[]{:S(2)}, u32[]{:S(2)}) collective-permute-start(bf16[256,256]{0,1:T(8,128)(2,1)S(1)} %bitcast.381), channel_id=1, source_target_pairs={{0,496},{16,0},{32,16},{48,32},{64,48},{80,64},{96,80},{112,96},{1... | collective-permute-start | bytes 393224 | tf_op jit(solution)/shard_map/ppermute | solution.py:14
  32.9 156.6 %copy-start.25 = (pred[16]{0:T(512)(128)(4,1)}, pred[16]{0:T(512)(128)(4,1)S(1)}, u32[]{:S(2)}) copy-start(pred[16]{0:T(512)(128)(4,1)S(1)} %compare_and_fusion) | copy-start | bytes 52
  115.6 69.5 %copy-start.1 = (bf16[1,1,4,256,256]{4,3,2,1,0:T(8,128)(2,1)S(1)}, bf16[1,1,4,256,256]{4,3,2,1,0:T(8,128)(2,1)}, u32[]{:S(2)}) copy-start(bf16[1,1,4,256,256]{4,3,2,1,0:T(8,128)(2,1)} %param.12) | copy-start | bytes 1572868
  165.3 273.1 %copy-start.24 = (s32[1,1,16]{2,1,0:T(1,128)S(1)}, s32[1,1,16]{2,1,0:T(1,128)}, u32[]{:S(2)}) copy-start(s32[1,1,16]{2,1,0:T(1,128)} %param.15) | copy-start | bytes 196
  165.4 19.1 %collective-permute-start.2 = (bf16[128,256]{0,1:T(8,128)(2,1)S(1)}, bf16[128,256]{0,1:T(8,128)(2,1)S(1)}, u32[]{:S(2)}, u32[]{:S(2)}) collective-permute-start(bf16[128,256]{0,1:T(8,128)(2,1)S(1)} %get-tuple-element.127), channel_id=1, source_target_pairs={{0,16},{16,32},{32,48},{48,64},{64,80},{80,96},{96,112},{112,128},... | collective-permute-start | bytes 196616 | tf_op jit(solution)/shard_map/ppermute | solution.py:14
  167.3 17.1 %collective-permute-start.3 = (bf16[128,256]{0,1:T(8,128)(2,1)S(1)}, bf16[128,256]{0,1:T(8,128)(2,1)S(1)}, u32[]{:S(2)}, u32[]{:S(2)}) collective-permute-start(bf16[128,256]{0,1:T(8,128)(2,1)S(1)} %get-tuple-element.128), channel_id=1, source_target_pairs={{0,1},{1,2},{2,3},{3,4},{4,5},{5,6},{6,7},{7,8},{8,9},{9,10},{10,1... | collective-permute-start | bytes 196616 | tf_op jit(solution)/shard_map/ppermute | solution.py:14
  327.9 562.2 %reduce-scatter.9.cloned.1.call-start = ((), (), s32[]{:S(2)}) async-start(), calls=%async_computation.3 | async-start | bytes 139264
  441.6 19.7 %collective-permute-start.4 = (f32[128,256]{1,0:T(8,128)S(1)}, f32[128,256]{1,0:T(8,128)S(1)}, u32[]{:S(2)}, u32[]{:S(2)}) collective-permute-start(f32[128,256]{1,0:T(8,128)S(1)} %get-tuple-element.115), channel_id=1, source_target_pairs={{0,496},{16,0},{32,16},{48,32},{64,48},{80,64},{96,80},{112,96},{1... | collective-permute-start | bytes 393224 | tf_op jit(solution)/shard_map/ppermute | solution.py:14
  457.4 6.7 collective-permute-start.5
  466.4 42.6 %copy-start.5 = (f32[128,2,256]{0,2,1:T(8,128)}, f32[128,2,256]{0,2,1:T(8,128)S(1)}, u32[]{:S(2)}) copy-start(f32[128,2,256]{0,2,1:T(8,128)S(1)} %get-tuple-element.90) | copy-start | bytes 786436
  466.5 18.8 %collective-permute-start.6 = (bf16[128,256]{0,1:T(8,128)(2,1)S(1)}, bf16[128,256]{0,1:T(8,128)(2,1)S(1)}, u32[]{:S(2)}, u32[]{:S(2)}) collective-permute-start(bf16[128,256]{0,1:T(8,128)(2,1)S(1)} %get-tuple-element.125), channel_id=1, source_target_pairs={{0,16},{16,32},{32,48},{48,64},{64,80},{80,96},{96,112},{112,128},... | collective-permute-start | bytes 196616 | tf_op jit(solution)/shard_map/ppermute | solution.py:14
  468.4 16.8 %collective-permute-start.7 = (bf16[128,256]{0,1:T(8,128)(2,1)S(1)}, bf16[128,256]{0,1:T(8,128)(2,1)S(1)}, u32[]{:S(2)}, u32[]{:S(2)}) collective-permute-start(bf16[128,256]{0,1:T(8,128)(2,1)S(1)} %get-tuple-element.126), channel_id=1, source_target_pairs={{0,1},{1,2},{2,3},{3,4},{4,5},{5,6},{6,7},{7,8},{8,9},{9,10},{10,1... | collective-permute-start | bytes 196616 | tf_op jit(solution)/shard_map/ppermute | solution.py:14
  486.3 21.0 %collective-permute-start.8 = (f32[128,256]{0,1:T(8,128)S(1)}, f32[128,256]{0,1:T(8,128)S(1)}, u32[]{:S(2)}, u32[]{:S(2)}) collective-permute-start(f32[128,256]{0,1:T(8,128)S(1)} %get-tuple-element.111), channel_id=1, source_target_pairs={{0,496},{16,0},{32,16},{48,32},{64,48},{80,64},{96,80},{112,96},{1... | collective-permute-start | bytes 393224 | tf_op jit(solution)/shard_map/ppermute | solution.py:14
  495.4 12.9 %collective-permute-start.9 = (f32[128,256]{0,1:T(8,128)S(1)}, f32[128,256]{0,1:T(8,128)S(1)}, u32[]{:S(2)}, u32[]{:S(2)}) collective-permute-start(f32[128,256]{0,1:T(8,128)S(1)} %get-tuple-element.112), channel_id=1, source_target_pairs={{0,15},{1,0},{2,1},{3,2},{4,3},{5,4},{6,5},{7,6},{8,7},{9,8},{10,9... | collective-permute-start | bytes 393224 | tf_op jit(solution)/shard_map/ppermute | solution.py:14
  509.0 105.4 %copy-start.7 = (f32[128,1,256]{0,2,1:T(8,128)}, f32[128,1,256]{0,2,1:T(8,128)S(1)}, u32[]{:S(2)}) copy-start(f32[128,1,256]{0,2,1:T(8,128)S(1)} %get-tuple-element.98) | copy-start | bytes 393220
  616.4 18.1 %collective-permute-start.10 = (bf16[128,256]{0,1:T(8,128)(2,1)S(1)}, bf16[128,256]{0,1:T(8,128)(2,1)S(1)}, u32[]{:S(2)}, u32[]{:S(2)}) collective-permute-start(bf16[128,256]{0,1:T(8,128)(2,1)S(1)} %get-tuple-element.123), channel_id=1, source_target_pairs={{0,16},{16,32},{32,48},{48,64},{64,80},{80,96},{96,112},{112,128},... | collective-permute-start | bytes 196616 | tf_op jit(solution)/shard_map/ppermute | solution.py:14
  618.3 16.2 %collective-permute-start.11 = (bf16[128,256]{0,1:T(8,128)(2,1)S(1)}, bf16[128,256]{0,1:T(8,128)(2,1)S(1)}, u32[]{:S(2)}, u32[]{:S(2)}) collective-permute-start(bf16[128,256]{0,1:T(8,128)(2,1)S(1)} %get-tuple-element.124), channel_id=1, source_target_pairs={{0,1},{1,2},{2,3},{3,4},{4,5},{5,6},{6,7},{7,8},{8,9},{9,10},{10,1... | collective-permute-start | bytes 196616 | tf_op jit(solution)/shard_map/ppermute | solution.py:14
  894.6 25.0 %copy-start.3 = (f32[1,1,128,2,256]{2,4,3,1,0:T(8,128)S(1)}, f32[1,1,128,2,256]{2,4,3,1,0:T(8,128)}, u32[]{:S(2)}) copy-start(f32[1,1,128,2,256]{2,4,3,1,0:T(8,128)} %copy.152) | copy-start | bytes 786436
  894.6 25.0 %copy-start.8 = (f32[128,1,256]{0,2,1:T(8,128)S(1)}, f32[128,1,256]{0,2,1:T(8,128)}, u32[]{:S(2)}) copy-start(f32[128,1,256]{0,2,1:T(8,128)} %copy-done.7) | copy-start | bytes 393220
  894.6 19.9 %collective-permute-start.12 = (f32[128,256]{1,0:T(8,128)S(1)}, f32[128,256]{1,0:T(8,128)S(1)}, u32[]{:S(2)}, u32[]{:S(2)}) collective-permute-start(f32[128,256]{1,0:T(8,128)S(1)} %get-tuple-element.109), channel_id=1, source_target_pairs={{0,496},{16,0},{32,16},{48,32},{64,48},{80,64},{96,80},{112,96},{1... | collective-permute-start | bytes 393224 | tf_op jit(solution)/shard_map/ppermute | solution.py:14
  910.6 6.8 collective-permute-start.13
  917.5 109.5 %copy-start.26 = (f32[128]{0:T(128)S(1)}, f32[128]{0:T(128)}, u32[]{:S(2)}) copy-start(f32[128]{0:T(128)} %get-tuple-element.85) | copy-start | bytes 1540
  1027.9 18.0 %collective-permute-start.14 = (bf16[128,256]{0,1:T(8,128)(2,1)S(1)}, bf16[128,256]{0,1:T(8,128)(2,1)S(1)}, u32[]{:S(2)}, u32[]{:S(2)}) collective-permute-start(bf16[128,256]{0,1:T(8,128)(2,1)S(1)} %get-tuple-element.121), channel_id=1, source_target_pairs={{0,16},{16,32},{32,48},{48,64},{64,80},{80,96},{96,112},{112,128},... | collective-permute-start | bytes 196616 | tf_op jit(solution)/shard_map/ppermute | solution.py:14
  1029.9 16.1 %collective-permute-start.15 = (bf16[128,256]{0,1:T(8,128)(2,1)S(1)}, bf16[128,256]{0,1:T(8,128)(2,1)S(1)}, u32[]{:S(2)}, u32[]{:S(2)}) collective-permute-start(bf16[128,256]{0,1:T(8,128)(2,1)S(1)} %get-tuple-element.122), channel_id=1, source_target_pairs={{0,1},{1,2},{2,3},{3,4},{4,5},{5,6},{6,7},{7,8},{8,9},{9,10},{10,1... | collective-permute-start | bytes 196616 | tf_op jit(solution)/shard_map/ppermute | solution.py:14
  1047.0 128.6 %copy-start.4 = (f32[1,1,128,2,256]{2,4,3,1,0:T(8,128)S(1)}, f32[1,1,128,2,256]{2,4,3,1,0:T(8,128)}, u32[]{:S(2)}) copy-start(f32[1,1,128,2,256]{2,4,3,1,0:T(8,128)} %copy.152) | copy-start | bytes 786436
  1047.1 128.6 %copy-start.18 = (f32[1,1,128,1,256]{2,4,3,1,0:T(8,128)S(1)}, f32[1,1,128,1,256]{2,4,3,1,0:T(8,128)}, u32[]{:S(2)}) copy-start(f32[1,1,128,1,256]{2,4,3,1,0:T(8,128)} %get-tuple-element.97) | copy-start | bytes 393220
  1047.1 128.5 %copy-start.19 = (f32[1,1,128,1,256]{2,4,3,1,0:T(8,128)S(1)}, f32[1,1,128,1,256]{2,4,3,1,0:T(8,128)}, u32[]{:S(2)}) copy-start(f32[1,1,128,1,256]{2,4,3,1,0:T(8,128)} %get-tuple-element.104) | copy-start | bytes 393220
  1047.1 16.8 %collective-permute-start.16 = (f32[128,256]{0,1:T(8,128)S(1)}, f32[128,256]{0,1:T(8,128)S(1)}, u32[]{:S(2)}, u32[]{:S(2)}) collective-permute-start(f32[128,256]{0,1:T(8,128)S(1)} %get-tuple-element.105), channel_id=1, source_target_pairs={{0,496},{16,0},{32,16},{48,32},{64,48},{80,64},{96,80},{112,96},{1... | collective-permute-start | bytes 393224 | tf_op jit(solution)/shard_map/ppermute | solution.py:14
  1052.0 13.2 %collective-permute-start.17 = (f32[128,256]{0,1:T(8,128)S(1)}, f32[128,256]{0,1:T(8,128)S(1)}, u32[]{:S(2)}, u32[]{:S(2)}) collective-permute-start(f32[128,256]{0,1:T(8,128)S(1)} %get-tuple-element.106), channel_id=1, source_target_pairs={{0,15},{1,0},{2,1},{3,2},{4,3},{5,4},{6,5},{7,6},{8,7},{9,8},{10,9... | collective-permute-start | bytes 393224 | tf_op jit(solution)/shard_map/ppermute | solution.py:14
  (15 other events, 159.6 us)
Sparse Core Ops, SparseCore 0:
  328.0 108.9 reduce-scatter.6
  779.2 110.7 reduce-scatter.8
where the time goes:
time: 1190 us; the launch traced here: 1180 us
  blocking collectives  588 us (49%)
  waiting for transfers between devices  286 us (24%)
  starting transfers between devices  121 us (10%)
  other arithmetic  119 us (10%)
  local copies, waits for them, and re-layouts  28.5 us (2%)
  matrix products  26.4 us (2%)
  between operations  15 us (1%)
    psum x3, blocking collectives, total_sum(): return lax.psum(value, ('slab', 'patch'))  318 us
    all_gather x2, blocking collectives, coarse_term(): gathered = lax.all_gather(coarse_rhs, 'slab', axis=0, tiled=True)  270 us
    unnamed x4, waiting for transfers between devices  217 us
    ppermute x18, starting transfers between devices, from_behind(): lax.ppermute(value, axis, [(i, (i + by) % count) for i in range(count)])  121 us
    ppermute x18, waiting for transfers between devices, from_behind(): lax.ppermute(value, axis, [(i, (i + by) % count) for i in range(count)])  68.9 us
    another operation x12, other arithmetic, on_device(): factors = jnp.linalg.cholesky(jnp.stack(face_sums))  67.7 us
    another operation x5, other arithmetic, face_solve(): jax.scipy.linalg.solve_triangular(factors, middle, lower=True, trans=1)  40.3 us
  transfers between devices with their start and end apart: 20, of which 11 were waited for; matrix products, arithmetic and copies ran while one was open for 1% of the time, Pallas kernels for 0%

commit v1 on v0

v1 whole, which is shorter than its diff:
```python
import jax
import jax.numpy as jnp
from jax import lax
from jax.experimental import pallas as pl
from jax.experimental.pallas import tpu as pltpu
from jax.sharding import Mesh, PartitionSpec as P

F = 256
NI = 1024
RHS = 128
PRIM = 16
OWN = 2 * F
SLAB = ("zh", "y", "x")
PATCH = ("zl", "core")
COLUMN = ("zh", "zl", "core")
PLANE = ("y", "x")
HIGHEST = lax.Precision.HIGHEST
ROUGH_STEPS = 12
FINE_STEPS = 64
VMEM = pl.BlockSpec(memory_space=pltpu.VMEM)
SMEM = pl.BlockSpec(memory_space=pltpu.SMEM)


def odd_pairs(count):
    return [(i, i ^ 1) for i in range(count)]


def even_pairs(count):
    return [(i, (i + 1) % count if i % 2 else (i - 1) % count) for i in range(count)]


def roll_pairs(count, by):
    return [(i, (i + by) % count) for i in range(count)]


def call(kernel, out_shapes, in_specs, name, flops=0, scratch=()):
    return pl.pallas_call(
        kernel,
        out_shape=out_shapes,
        in_specs=in_specs,
        out_specs=jax.tree.map(lambda _: VMEM, out_shapes),
        scratch_shapes=list(scratch),
        compiler_params=pltpu.CompilerParams(vmem_limit_bytes=16 * 1024 * 1024),
        cost_estimate=pl.CostEstimate(flops=flops, bytes_accessed=1 << 20, transcendentals=0),
        name=name,
    )


def f32(*shape):
    return jax.ShapeDtypeStruct(shape, jnp.float32)


def bf16(*shape):
    return jax.ShapeDtypeStruct(shape, jnp.bfloat16)


def fine_dot(a, b):
    return jnp.dot(a, b, precision=HIGHEST, preferred_element_type=jnp.float32)


def rough_dot(a, b):
    return jnp.dot(a, b, preferred_element_type=jnp.float32)


def rows(number):
    return slice(number * F, (number + 1) * F)


def prepare_kernel(even_ref, rhs_ref, blocks_ref, slab_b, first_ref, patch_b, slab_a, patch_a, second_ref):
    for even, ahead, back, a_ref, b_ref in ((even_ref[0], 0, 2, slab_a, slab_b), (even_ref[1], 1, 3, patch_a, patch_b)):
        @pl.when(even == 1)
        def _():
            b_ref[...] = blocks_ref[back]
            a_ref[...] = blocks_ref[ahead]

        @pl.when(even == 0)
        def _():
            b_ref[...] = blocks_ref[ahead]
            a_ref[...] = blocks_ref[back]

    first_ref[...] = rhs_ref[:, 0, :].T
    second_ref[...] = rhs_ref[:, 1, :].T


def primal_kernel(ids_ref, blocks_ref, primal_ref):
    row = lax.broadcasted_iota(jnp.int32, (PRIM, NI), 0)
    picked = jnp.zeros((PRIM, NI), jnp.int32)
    for k in range(PRIM):
        picked = jnp.where(row == k, ids_ref[k], picked)
    onehot = (picked == lax.broadcasted_iota(jnp.int32, (PRIM, NI), 1)).astype(jnp.float32).astype(jnp.bfloat16)
    for f in range(4):
        primal_ref[:, rows(f)] = rough_dot(onehot[:, rows(f)], blocks_ref[f]).astype(jnp.bfloat16)


def invert_kernel(even_ref, blocks_ref, slab_b, patch_b, slab_a, patch_a, out_ref, a_ref):
    index = lax.broadcasted_iota(jnp.int32, (F, F), 0)
    unit = (index == lax.broadcasted_iota(jnp.int32, (F, F), 1)).astype(jnp.float32)

    def start(f):
        bound = jnp.max(jnp.sum(jnp.abs(a_ref[f]), axis=0, keepdims=True), axis=1, keepdims=True)
        return unit * (1.9 / bound)

    for f in range(4):
        b, a = ((slab_b, slab_a), (patch_b, patch_a))[f % 2]
        other = jnp.where(even_ref[f % 2] == (1 if f < 2 else 0), a[...], b[...])
        a_ref[f] = blocks_ref[f].astype(jnp.float32) + other.astype(jnp.float32)
        out_ref[f] = start(f)

    def newton(multiply):
        lefts = [unit - multiply(a_ref[f], out_ref[f]) for f in range(4)]
        worst = jnp.float32(0.0)
        for f in range(4):
            worst = jnp.maximum(worst, jnp.sum(lefts[f] * lefts[f]))
        for f in range(4):
            out_ref[f] = out_ref[f] + multiply(out_ref[f], lefts[f])
        return worst

    def rough(a, b):
        return rough_dot(a.astype(jnp.bfloat16), b.astype(jnp.bfloat16))

    def rough_body(carry):
        step, _ = carry
        return step + 1, newton(rough)

    _, worst = lax.while_loop(lambda c: (c[0] < ROUGH_STEPS) & ~(c[1] < 0.25), rough_body, (0, jnp.float32(1e30)))

    @pl.when(~(worst < 0.25))
    def _():
        for f in range(4):
            out_ref[f] = start(f)

    def fine_body(carry):
        step, last, _ = carry
        return step + 1, newton(fine_dot), last

    lax.while_loop(
        lambda c: (c[0] < FINE_STEPS) & (c[1] > 1e-6) & ~((c[1] < 1e-2) & (c[1] >= c[2])),
        fine_body, (0, jnp.float32(1e30), jnp.float32(1e31)))


def solve_and_restrict(residual_of, factors_ref, primal_ref, lifted_ref, rounded_ref, c_ref):
    for f in range(4):
        lifted = fine_dot(factors_ref[f], residual_of(f))
        lifted_ref[rows(f)] = lifted
        rounded_ref[rows(f)] = lifted.astype(jnp.bfloat16)
    c = rough_dot(primal_ref[...], rounded_ref[...]).astype(jnp.bfloat16)
    for j in range(32):
        c_ref[j] = c


def first_kernel(own_ref, second_ref, slab_ref, patch_ref, factors_ref, primal_ref, residual_ref, lifted_ref, rounded_ref, c_ref):
    residual_ref[rows(0)] = own_ref[...]
    residual_ref[rows(1)] = second_ref[...]
    residual_ref[rows(2)] = slab_ref[...]
    residual_ref[rows(3)] = patch_ref[...]
    solve_and_restrict(lambda f: residual_ref[rows(f)], factors_ref, primal_ref, lifted_ref, rounded_ref, c_ref)


def write_parts(even_ref, terms_ref, outs):
    slab_b, patch_b, slab_a, patch_a = outs
    for even, ahead, back, a_ref, b_ref in ((even_ref[0], 0, 2, slab_a, slab_b), (even_ref[1], 1, 3, patch_a, patch_b)):
        upper, lower = terms_ref[rows(ahead)], terms_ref[rows(back)]
        b_ref[...] = jnp.where(even == 1, lower, upper)
        a_ref[...] = jnp.where(even == 1, upper, lower)


def assembled(even_ref, terms_ref, got, f):
    slab_b, patch_b, slab_a, patch_a = got
    a_ref, b_ref = ((slab_a, slab_b), (patch_a, patch_b))[f % 2]
    use_a = even_ref[f % 2] == (1 if f < 2 else 0)
    return terms_ref[rows(f)] + jnp.where(use_a, a_ref[...], b_ref[...])


def coarse_kernel(coarse_ref, gathered_ref, out_ref):
    gathered = gathered_ref[...].reshape(OWN, RHS)
    out_ref[...] = rough_dot(coarse_ref[...], gathered).reshape(16, PRIM, RHS)


def repeat_rows(out_ref, value):
    for j in range(out_ref.shape[0]):
        out_ref[j] = value


def sum_kernel(parts_ref, out_ref):
    repeat_rows(out_ref, jnp.sum(parts_ref[...], axis=0))


def terms_kernel(even_ref, parts_ref, inverse_ref, rounded_ref, primal_ref, residual_ref, lifted_ref, terms_ref,
                 product_ref, *outs):
    u = jnp.sum(parts_ref[...], axis=0).astype(jnp.bfloat16)
    product = jnp.zeros((1, RHS), jnp.float32)
    for f in range(4):
        term = rough_dot(inverse_ref[rows(f)], rounded_ref[...]) + lax.dot_general(
            primal_ref[:, rows(f)], u, (((0,), (0,)), ((), ())), preferred_element_type=jnp.float32)
        terms_ref[rows(f)] = term
        lifted = lifted_ref[rows(f)]
        weight = term + residual_ref[rows(f)] if f < 2 else term
        product = product + jnp.sum(lifted * weight, axis=0, keepdims=True)
    repeat_rows(product_ref, product)
    write_parts(even_ref, terms_ref, outs)


def direction_kernel(again, *refs):
    if again:
        sums_ref, before_ref, last_ref, *refs = refs
        scale = jnp.sum(sums_ref[...], axis=0) / jnp.sum(before_ref[...], axis=0)[:1]
    else:
        over_ref, *refs = refs
    (even_ref, terms_ref, slab_b, patch_b, slab_a, patch_a, lifted_ref, factors_ref, blocks_ref, inverse_ref,
     direction_ref, image_ref, product_ref, *outs, rounded_ref) = refs
    got = (slab_b, patch_b, slab_a, patch_a)
    for f in range(4):
        value = lifted_ref[rows(f)] + fine_dot(factors_ref[f], assembled(even_ref, terms_ref, got, f))
        if again:
            value = value + scale * last_ref[rows(f)]
        direction_ref[rows(f)] = value
        rounded_ref[rows(f)] = value.astype(jnp.bfloat16)
    product = jnp.zeros((1, RHS), jnp.float32)
    for f in range(4):
        image = rough_dot(blocks_ref[f], rounded_ref[rows(f)]) - rough_dot(inverse_ref[rows(f)], rounded_ref[...])
        image_ref[rows(f)] = image
        product = product + jnp.sum(direction_ref[rows(f)] * image, axis=0, keepdims=True)
    repeat_rows(product_ref, product if again else jnp.concatenate([over_ref[0], product], axis=0))
    if again:
        outs[0][...] = image_ref[rows(2)]
        outs[1][...] = image_ref[rows(3)]
    else:
        write_parts(even_ref, image_ref, outs)


def update_kernel(even_ref, sums_ref, image_ref, slab_b, patch_b, slab_a, patch_a, last_ref, factors_ref, primal_ref,
                  residual_ref, lifted_ref, rounded_ref, c_ref):
    sums = jnp.sum(sums_ref[...], axis=0)
    step = sums[:1] / sums[1:]
    got = (slab_b, patch_b, slab_a, patch_a)
    for f in range(4):
        residual_ref[rows(f)] = last_ref[rows(f)] - step * assembled(even_ref, image_ref, got, f)
    solve_and_restrict(lambda f: residual_ref[rows(f)], factors_ref, primal_ref, lifted_ref, rounded_ref, c_ref)


def last_kernel(first_ref, over_ref, under_ref, first_direction_ref, direction_ref, residual_ref, image_ref,
                slab_ref, patch_ref, solution_ref, out_ref):
    first = jnp.sum(first_ref[...], axis=0)
    first_step = first[:1] / first[1:]
    step = jnp.sum(over_ref[...], axis=0) / jnp.sum(under_ref[...], axis=0)
    for f, got in ((0, slab_ref), (1, patch_ref)):
        value = first_step * first_direction_ref[rows(f)] + step * direction_ref[rows(f)]
        left = residual_ref[rows(f)] - step * (image_ref[rows(f)] + got[...])
        solution_ref[:, f, :] = value.T
        out_ref[:, f, :] = left.T


def swap(parts):
    slab_b, patch_b, slab_a, patch_a = parts
    return (
        lax.ppermute(slab_b, SLAB, even_pairs(32)),
        lax.ppermute(patch_b, PATCH, even_pairs(16)),
        lax.ppermute(slab_a, SLAB, odd_pairs(32)),
        lax.ppermute(patch_a, PATCH, odd_pairs(16)),
    )


def total_parts(spread):
    parts = lax.all_to_all(spread, COLUMN, 0, 0)
    spread = call(sum_kernel, f32(16, *spread.shape[1:]), [VMEM], "sum")(parts)
    return lax.all_to_all(spread, PLANE, 0, 0)


def on_device(rhs, face_blocks, interior_inverse, coarse_inverse, primal_ids):
    blocks = face_blocks[0, 0]
    inverse = interior_inverse[0, 0]
    ids = primal_ids[0, 0]
    slab_even = 1 - lax.axis_index("x") % 2
    patch_even = 1 - lax.axis_index("core")
    even = jnp.stack([slab_even, patch_even]).astype(jnp.int32)

    slab_b, first, patch_b, slab_a, patch_a, second = call(
        prepare_kernel, [bf16(F, F), f32(F, RHS)] + [bf16(F, F)] * 3 + [f32(F, RHS)], [SMEM, VMEM, VMEM], "prepare")(
            even, rhs[0, 0], blocks)
    slab_b = lax.ppermute(slab_b, SLAB, even_pairs(32))
    from_slab = lax.ppermute(first, SLAB, roll_pairs(32, 1))
    patch_b = lax.ppermute(patch_b, PATCH, even_pairs(16))
    slab_a = lax.ppermute(slab_a, SLAB, odd_pairs(32))
    patch_a = lax.ppermute(patch_a, PATCH, odd_pairs(16))
    from_patch = lax.ppermute(second, PATCH, roll_pairs(16, 1))
    primal = call(primal_kernel, bf16(PRIM, NI), [SMEM, VMEM], "primal")(ids, blocks)
    slab_b, from_slab, patch_b, slab_a, patch_a, from_patch = lax.optimization_barrier(
        (slab_b, from_slab, patch_b, slab_a, patch_a, from_patch))
    got = (slab_b, patch_b, slab_a, patch_a)

    factors = call(invert_kernel, f32(4, F, F), [SMEM] + [VMEM] * 5, "invert", 4 * 16 * 2 * F ** 3,
                   [pltpu.VMEM((4, F, F), jnp.float32)])(even, blocks, *got)

    field = f32(NI, RHS)
    part = [f32(F, RHS)] * 4
    solved = [field, field, bf16(NI, RHS), bf16(32, PRIM, RHS)]
    solve_flops = 4 * 12 * F * F * RHS

    def coarse_terms(residual, lifted, rounded, c):
        gathered = lax.all_to_all(c, SLAB, 0, 0)
        partial = call(coarse_kernel, f32(16, PRIM, RHS), [VMEM] * 2, "coarse", 1 << 25)(coarse_inverse, gathered)
        parts = lax.all_to_all(partial, PATCH, 0, 0)
        terms, product, *send = call(
            terms_kernel, [field, f32(32, 1, RHS)] + part, [SMEM] + [VMEM] * 6, "terms", 1 << 28)(
                even, parts, inverse, rounded, primal, residual, lifted)
        return terms, product, send

    scratch = [pltpu.VMEM((NI, RHS), jnp.bfloat16)]
    residual, lifted, rounded, c = call(first_kernel, solved, [VMEM] * 6, "first", solve_flops)(
        first, second, from_slab, from_patch, factors, primal)
    terms, product, send = coarse_terms(residual, lifted, rounded, c)
    got = swap(send)
    first_direction, image, spread, *send = call(
        lambda *refs: direction_kernel(False, *refs), [field, field, f32(32, 2, RHS)] + part,
        [VMEM, SMEM] + [VMEM] * 9, "direction", solve_flops, scratch)(
            product, even, terms, *got, lifted, factors, blocks, inverse)

    got = swap(send)
    first_sums = total_parts(spread)
    first_sums, got = lax.optimization_barrier((first_sums, got))
    residual, lifted, rounded, c = call(update_kernel, solved, [SMEM] + [VMEM] * 9, "update", solve_flops)(
        even, first_sums, image, *got, residual, factors, primal)
    terms, spread, send = coarse_terms(residual, lifted, rounded, c)
    got = swap(send)
    over = total_parts(spread)
    over, got = lax.optimization_barrier((over, got))
    direction, image, spread, *send = call(
        lambda *refs: direction_kernel(True, *refs), [field, field, f32(32, 1, RHS)] + part[:2],
        [VMEM] * 3 + [SMEM] + [VMEM] * 9, "direction_again", solve_flops, scratch)(
            over, first_sums, first_direction, even, terms, *got, lifted, factors, blocks, inverse)

    from_slab = lax.ppermute(send[0], SLAB, roll_pairs(32, -1))
    from_patch = lax.ppermute(send[1], PATCH, roll_pairs(16, -1))
    under = total_parts(spread)
    under, from_slab, from_patch = lax.optimization_barrier((under, from_slab, from_patch))
    solution, residual = call(last_kernel, [f32(RHS, 2, F)] * 2, [VMEM] * 9, "last")(
        first_sums, over, under, first_direction, direction, residual, image, from_slab, from_patch)
    return (solution.reshape(1, 1, RHS, 2, F), residual.reshape(1, 1, RHS, 2, F))


def solution(mesh):
    chips = Mesh(mesh.devices.reshape(2, 4, 4, 8, 2), ("zh", "y", "x", "zl", "core"))
    return jax.shard_map(
        on_device,
        mesh=chips,
        in_specs=(
            P(SLAB, PATCH, None, None, None),
            P(SLAB, PATCH, None, None, None),
            P(SLAB, PATCH, None, None),
            P(SLAB, PATCH),
            P(SLAB, PATCH, None),
        ),
        out_specs=(P(SLAB, PATCH, None, None, None), P(SLAB, PATCH, None, None, None)),
        check_vma=False,
    )
```

time: 1190 us -> 328 us (0.28)
  blocking collectives: 588 us -> 153 us
  waiting for transfers between devices: 286 us -> 30.5 us
  other arithmetic: 119 us -> 0.08 us
  matrix products: 26.4 us -> 0 us
  Pallas kernels: 0 us -> 22.1 us
  local copies, waits for them, and re-layouts: 28.5 us -> 11.1 us
  between operations: 15 us -> 1.01 us
  starting transfers between devices: 121 us -> 109 us
    psum x3 -> x0, blocking collectives: 318 us -> none  [total_sum(): return lax.psum(value, ('slab', 'patch'))]
    all_gather x2 -> x0, blocking collectives: 270 us -> none  [coarse_term(): gathered = lax.all_gather(coarse_rhs, 'slab', axis=0, tiled=True)]
    unnamed x4 -> x0, waiting for transfers between devices: 217 us -> none
    all_to_all x0 -> x8, blocking collectives: none -> 153 us  [the longest x2 51.5 us: coarse_terms(): gathered = lax.all_to_all(c, SLAB, 0, 0)]
    another operation x25 -> x1, other arithmetic: 113 us -> 0.08 us  [on_device(): even = jnp.stack([slab_even, patch_even]).astype(jnp.int32)]
    ppermute x18 -> x20, waiting for transfers between devices: 68.9 us -> 26.8 us  [the longest x1 15.8 us: on_device(): from_slab = lax.ppermute(first, SLAB, roll_pairs(32, 1))]
    ppermute x18 -> x20, starting transfers between devices: 121 us -> 91.4 us  [the longest x3 21.9 us: swap(): lax.ppermute(slab_b, SLAB, even_pairs(32))]
    pallas_call x0 -> x15, Pallas kernels: none -> 22.1 us  [the longest x1 6.9 us: on_device(): call(invert_kernel, f32(4, F, F), [SMEM] + [VMEM] * 5, 'invert', 4 * 16 *...]
  transfers between devices with their start and end apart: 20 -> 22, of which waited for: 11 -> 4; matrix products, arithmetic and copies ran while one was open for 1% -> 0% of each run, Pallas kernels for 0% -> 0%
where the time goes in v1:
time: 328 us; the launch traced here: 327 us
  blocking collectives  153 us (47%)
  starting transfers between devices  109 us (33%)
  waiting for transfers between devices  30.5 us (9%)
  Pallas kernels  22.1 us (7%)
  local copies, waits for them, and re-layouts  11.1 us (3%)
    all_to_all x2, blocking collectives, coarse_terms(): gathered = lax.all_to_all(c, SLAB, 0, 0)  51.5 us
    all_to_all x2, blocking collectives, total_parts(): parts = lax.all_to_all(spread, COLUMN, 0, 0)  46.7 us
    all_to_all x2, blocking collectives, coarse_terms(): parts = lax.all_to_all(partial, PATCH, 0, 0)  33.8 us
    ppermute x3, starting transfers between devices, swap(): lax.ppermute(slab_b, SLAB, even_pairs(32))  21.9 us
    ppermute x1, starting transfers between devices, on_device(): slab_b = lax.ppermute(slab_b, SLAB, even_pairs(32))  20.9 us
    all_to_all x2, blocking collectives, total_parts(): return lax.all_to_all(spread, PLANE, 0, 0)  20.9 us
    ppermute x1, waiting for transfers between devices, on_device(): from_slab = lax.ppermute(first, SLAB, roll_pairs(32, 1))  15.8 us
    ppermute x3, starting transfers between devices, swap(): lax.ppermute(patch_a, PATCH, odd_pairs(16))  12.4 us
  transfers between devices with their start and end apart: 22, of which 4 were waited for; matrix products, arithmetic and copies ran while one was open for 0% of the time, Pallas kernels for 0%

profile of v1, /device:TPU:1, one launch (start us, length us, event | category | flops | bytes accessed | tf_op | source)
XLA Modules:
  0.0 326.7 jit_solution(14909772132700115749)
XLA Ops:
  3.5 20.9 %collective-permute-start = (bf16[256,256]{1,0:T(8,128)(2,1)S(1)}, bf16[256,256]{1,0:T(8,128)(2,1)S(1)}, u32[]{:S(2)}, u32[]{:S(2)}) collective-permute-start(bf16[256,256]{1,0:T(8,128)(2,1)S(1)} %get-tuple-element.63), channel_id=1, source_target_pairs={{0,496},{16,32},{32,16},{48,64},{64,48},{80,96},{96,80},{112,128},... | collective-permute-start | bytes 393224 | tf_op jit(solution)/shard_map/ppermute | solution.py:280
  24.4 3.5 %collective-permute-start.2 = (bf16[256,256]{1,0:T(8,128)(2,1)S(1)}, bf16[256,256]{1,0:T(8,128)(2,1)S(1)}, u32[]{:S(2)}, u32[]{:S(2)}) collective-permute-start(bf16[256,256]{1,0:T(8,128)(2,1)S(1)} %get-tuple-element.64), channel_id=1, source_target_pairs={{0,15},{1,2},{2,1},{3,4},{4,3},{5,6},{6,5},{7,8},{8,7},{9,10},{10,... | collective-permute-start | bytes 393224 | tf_op jit(solution)/shard_map/ppermute | solution.py:282
  29.8 4.2 %collective-permute-start.4 = (bf16[256,256]{1,0:T(8,128)(2,1)S(1)}, bf16[256,256]{1,0:T(8,128)(2,1)S(1)}, u32[]{:S(2)}, u32[]{:S(2)}) collective-permute-start(bf16[256,256]{1,0:T(8,128)(2,1)S(1)} %get-tuple-element.66), channel_id=1, source_target_pairs={{0,1},{1,0},{2,3},{3,2},{4,5},{5,4},{6,7},{7,6},{8,9},{9,8},{10,11... | collective-permute-start | bytes 393224 | tf_op jit(solution)/shard_map/ppermute | solution.py:284
  34.0 3.6 %collective-permute-start.1 = (f32[256,128]{1,0:T(8,128)S(1)}, f32[256,128]{1,0:T(8,128)S(1)}, u32[]{:S(2)}, u32[]{:S(2)}) collective-permute-start(f32[256,128]{1,0:T(8,128)S(1)} %get-tuple-element.61.own_ref), channel_id=1, source_target_pairs={{0,16},{16,32},{32,48},{48,64},{64,80},{80,96},{96,112},{112,128},... | collective-permute-start | bytes 393224 | tf_op jit(solution)/shard_map/ppermute | solution.py:281
  37.7 2.8 collective-permute-start.5
  42.9 15.8 %collective-permute-done.1.slab_ref = f32[256,128]{1,0:T(8,128)S(1)} collective-permute-done((f32[256,128]{1,0:T(8,128)S(1)}, f32[256,128]{1,0:T(8,128)S(1)}, u32[]{:S(2)}, u32[]{:S(2)}) %collective-permute-start.1) | collective-permute-done | bytes 131104 | tf_op jit(solution)/shard_map/ppermute | solution.py:281
  59.8 6.9 %invert.1.factors_ref.refs_8_.refs_10_ = f32[4,256,256]{2,1,0:T(8,128)S(1)} custom-call(s32[2]{0:T(128)S(1)} %pad_add_fusion.even_ref.refs_1_.refs_3_, bf16[4,256,256]{2,1,0:T(8,128)(2,1)S(1)} %bitcast.14, bf16[256,256]{1,0:T(8,128)(2,1)S(1)} %collective-permute-done.slab_b, bf16[256,256]{1,0:T(8,128)(2,1)S(1)} %collective-permute-done.2.patch_b, ...), custom_call_target="tpu_custom_call" | custom-call | flops 2147483648 | bytes 1048576 | tf_op jit(solution)/shard_map/invert/pallas_call | solution.py:291
  67.9 24.5 %all_to_all.50.gathered_ref = bf16[32,16,128]{2,1,0:T(8,128)(2,1)S(1)} all-to-all(bf16[32,16,128]{2,1,0:T(8,128)(2,1)S(1)} %get-tuple-element.73), channel_id=1, replica_groups=mesh['zh'=2,'y'=4,'x'=4,'zl'=8,'core'=2] {'zh','y','x'}, dimensions={0} | all-to-all | bytes 262144 | tf_op jit(solution)/shard_map/all_to_all | solution.py:300
  92.7 16.4 %all_to_all.51.parts_ref = f32[16,16,128]{2,1,0:T(8,128)S(1)} all-to-all(f32[16,16,128]{2,1,0:T(8,128)S(1)} %coarse.2), channel_id=1, replica_groups=mesh['zh'=2,'y'=4,'x'=4,'zl'=8,'core'=2] {'zl','core'}, dimensions={0} | all-to-all | bytes 262144 | tf_op jit(solution)/shard_map/all_to_all | solution.py:302
  110.5 4.6 %collective-permute-start.6 = (f32[256,128]{1,0:T(8,128)S(1)}, f32[256,128]{1,0:T(8,128)S(1)}, u32[]{:S(2)}, u32[]{:S(2)}) collective-permute-start(f32[256,128]{1,0:T(8,128)S(1)} %get-tuple-element.79), channel_id=1, source_target_pairs={{0,496},{16,32},{32,16},{48,64},{64,48},{80,96},{96,80},{112,128},... | collective-permute-start | bytes 393224 | tf_op jit(solution)/shard_map/ppermute | solution.py:256
  118.9 5.2 %collective-permute-start.9 = (f32[256,128]{1,0:T(8,128)S(1)}, f32[256,128]{1,0:T(8,128)S(1)}, u32[]{:S(2)}, u32[]{:S(2)}) collective-permute-start(f32[256,128]{1,0:T(8,128)S(1)} %get-tuple-element.82), channel_id=1, source_target_pairs={{0,1},{1,0},{2,3},{3,2},{4,5},{5,4},{6,7},{7,6},{8,9},{9,8},{10,11... | collective-permute-start | bytes 393224 | tf_op jit(solution)/shard_map/ppermute | solution.py:259
  124.1 8.3 %collective-permute-done.6.refs_3_ = f32[256,128]{1,0:T(8,128)S(1)} collective-permute-done((f32[256,128]{1,0:T(8,128)S(1)}, f32[256,128]{1,0:T(8,128)S(1)}, u32[]{:S(2)}, u32[]{:S(2)}) %collective-permute-start.6) | collective-permute-done | bytes 131104 | tf_op jit(solution)/shard_map/ppermute | solution.py:256
  132.5 2.9 direction.1
  139.7 11.9 %all-to-all-start.2 = ((f32[32,2,128]{2,1,0:T(2,128)}), f32[32,2,128]{2,1,0:T(2,128)S(1)}, u32[]{:S(2)}, u32[]{:S(2)}) async-start(f32[32,2,128]{2,1,0:T(2,128)} %get-tuple-element.83), calls=%async_computation.2 | async-start | bytes 65536 | tf_op jit(solution)/shard_map/all_to_all | solution.py:264
  151.6 13.5 %collective-permute-start.10 = (f32[256,128]{1,0:T(8,128)}, f32[256,128]{1,0:T(8,128)}, u32[]{:S(2)}, u32[]{:S(2)}) collective-permute-start(f32[256,128]{1,0:T(8,128)} %copy-done.18), channel_id=1, source_target_pairs={{0,496},{16,32},{32,16},{48,64},{64,48},{80,96},{96,80},{112,128},... | collective-permute-start | bytes 393224 | tf_op jit(solution)/shard_map/ppermute | solution.py:256
  165.1 2.7 collective-permute-start.11
  167.8 1.9 collective-permute-start.12
  172.3 5.7 %all-to-all-start.3 = ((f32[16,2,128]{2,1,0:T(2,128)}), f32[16,2,128]{2,1,0:T(2,128)S(1)}, u32[]{:S(2)}, u32[]{:S(2)}) async-start(f32[16,2,128]{2,1,0:T(2,128)} %sum.3), calls=%async_computation.3 | async-start | bytes 32768 | tf_op jit(solution)/shard_map/all_to_all | solution.py:266
  178.1 2.6 collective-permute-done.11.patch_b
  180.7 3.7 %all-to-all-done.3.sums_ref.refs_1_.first_ref = f32[16,2,128]{2,1,0:T(2,128)S(1)} async-done(((f32[16,2,128]{2,1,0:T(2,128)}), f32[16,2,128]{2,1,0:T(2,128)S(1)}, u32[]{:S(2)}, u32[]{:S(2)}) %all-to-all-start.3) | async-done | bytes 16416 | tf_op jit(solution)/shard_map/all_to_all | solution.py:266
  186.5 2.4 update.1
  188.9 27.0 %all_to_all.52.gathered_ref = bf16[32,16,128]{2,1,0:T(8,128)(2,1)S(1)} all-to-all(bf16[32,16,128]{2,1,0:T(8,128)(2,1)S(1)} %get-tuple-element.94), channel_id=1, replica_groups=mesh['zh'=2,'y'=4,'x'=4,'zl'=8,'core'=2] {'zh','y','x'}, dimensions={0} | all-to-all | bytes 262144 | tf_op jit(solution)/shard_map/all_to_all | solution.py:300
  216.0 17.4 %all_to_all.53.parts_ref = f32[16,16,128]{2,1,0:T(8,128)S(1)} all-to-all(f32[16,16,128]{2,1,0:T(8,128)S(1)} %coarse.3), channel_id=1, replica_groups=mesh['zh'=2,'y'=4,'x'=4,'zl'=8,'core'=2] {'zl','core'}, dimensions={0} | all-to-all | bytes 262144 | tf_op jit(solution)/shard_map/all_to_all | solution.py:302
  234.8 3.8 %collective-permute-start.14 = (f32[256,128]{1,0:T(8,128)S(1)}, f32[256,128]{1,0:T(8,128)S(1)}, u32[]{:S(2)}, u32[]{:S(2)}) collective-permute-start(f32[256,128]{1,0:T(8,128)S(1)} %get-tuple-element.99), channel_id=1, source_target_pairs={{0,496},{16,32},{32,16},{48,64},{64,48},{80,96},{96,80},{112,128},... | collective-permute-start | bytes 393224 | tf_op jit(solution)/shard_map/ppermute | solution.py:256
  242.4 5.3 %collective-permute-start.17 = (f32[256,128]{1,0:T(8,128)S(1)}, f32[256,128]{1,0:T(8,128)S(1)}, u32[]{:S(2)}, u32[]{:S(2)}) collective-permute-start(f32[256,128]{1,0:T(8,128)S(1)} %get-tuple-element.102), channel_id=1, source_target_pairs={{0,1},{1,0},{2,3},{3,2},{4,5},{5,4},{6,7},{7,6},{8,9},{9,8},{10,11... | collective-permute-start | bytes 393224 | tf_op jit(solution)/shard_map/ppermute | solution.py:259
  247.7 23.3 %all_to_all.54.parts_ref = f32[32,1,128]{2,1,0:T(1,128)S(1)} all-to-all(f32[32,1,128]{2,1,0:T(1,128)S(1)} %get-tuple-element.98), channel_id=1, replica_groups=mesh['zh'=2,'y'=4,'x'=4,'zl'=8,'core'=2] {'zh','zl','core'}, dimensions={0} | all-to-all | bytes 32768 | tf_op jit(solution)/shard_map/all_to_all | solution.py:264
  271.1 11.9 %all_to_all.55.refs_0_.over_ref = f32[16,1,128]{2,1,0:T(1,128)S(1)} all-to-all(f32[16,1,128]{2,1,0:T(1,128)S(1)} %sum.4), channel_id=1, replica_groups=mesh['zh'=2,'y'=4,'x'=4,'zl'=8,'core'=2] {'y','x'}, dimensions={0} | all-to-all | bytes 16384 | tf_op jit(solution)/shard_map/all_to_all | solution.py:266
  283.1 2.3 direction_again.1
  285.4 3.6 %collective-permute-start.18 = (f32[256,128]{1,0:T(8,128)S(1)}, f32[256,128]{1,0:T(8,128)S(1)}, u32[]{:S(2)}, u32[]{:S(2)}) collective-permute-start(f32[256,128]{1,0:T(8,128)S(1)} %get-tuple-element.111), channel_id=1, source_target_pairs={{0,496},{16,0},{32,16},{48,32},{64,48},{80,64},{96,80},{112,96},{1... | collective-permute-start | bytes 393224 | tf_op jit(solution)/shard_map/ppermute | solution.py:332
  289.0 4.3 %collective-permute-start.19 = (f32[256,128]{1,0:T(8,128)S(1)}, f32[256,128]{1,0:T(8,128)S(1)}, u32[]{:S(2)}, u32[]{:S(2)}) collective-permute-start(f32[256,128]{1,0:T(8,128)S(1)} %get-tuple-element.112), channel_id=1, source_target_pairs={{0,15},{1,0},{2,1},{3,2},{4,3},{5,4},{6,5},{7,6},{8,7},{9,8},{10,9... | collective-permute-start | bytes 393224 | tf_op jit(solution)/shard_map/ppermute | solution.py:333
  293.3 23.3 %all_to_all.56.parts_ref = f32[32,1,128]{2,1,0:T(1,128)S(1)} all-to-all(f32[32,1,128]{2,1,0:T(1,128)S(1)} %get-tuple-element.110), channel_id=1, replica_groups=mesh['zh'=2,'y'=4,'x'=4,'zl'=8,'core'=2] {'zh','zl','core'}, dimensions={0} | all-to-all | bytes 32768 | tf_op jit(solution)/shard_map/all_to_all | solution.py:264
  316.7 8.9 %all_to_all.57.under_ref = f32[16,1,128]{2,1,0:T(1,128)S(1)} all-to-all(f32[16,1,128]{2,1,0:T(1,128)S(1)} %sum.5), channel_id=1, replica_groups=mesh['zh'=2,'y'=4,'x'=4,'zl'=8,'core'=2] {'y','x'}, dimensions={0} | all-to-all | bytes 16384 | tf_op jit(solution)/shard_map/all_to_all | solution.py:266
  (74 shorter events, 30.3 us)
Async XLA Ops:
  0.7 1.0 copy-start.1
  3.5 34.2 %collective-permute-start = (bf16[256,256]{1,0:T(8,128)(2,1)S(1)}, bf16[256,256]{1,0:T(8,128)(2,1)S(1)}, u32[]{:S(2)}, u32[]{:S(2)}) collective-permute-start(bf16[256,256]{1,0:T(8,128)(2,1)S(1)} %get-tuple-element.63), channel_id=1, source_target_pairs={{0,496},{16,32},{32,16},{48,64},{64,48},{80,96},{96,80},{112,128},... | collective-permute-start | bytes 393224 | tf_op jit(solution)/shard_map/ppermute | solution.py:280
  24.4 18.5 %collective-permute-start.2 = (bf16[256,256]{1,0:T(8,128)(2,1)S(1)}, bf16[256,256]{1,0:T(8,128)(2,1)S(1)}, u32[]{:S(2)}, u32[]{:S(2)}) collective-permute-start(bf16[256,256]{1,0:T(8,128)(2,1)S(1)} %get-tuple-element.64), channel_id=1, source_target_pairs={{0,15},{1,2},{2,1},{3,4},{4,3},{5,6},{6,5},{7,8},{8,7},{9,10},{10,... | collective-permute-start | bytes 393224 | tf_op jit(solution)/shard_map/ppermute | solution.py:282
  27.9 15.0 %collective-permute-start.3 = (bf16[256,256]{1,0:T(8,128)(2,1)S(1)}, bf16[256,256]{1,0:T(8,128)(2,1)S(1)}, u32[]{:S(2)}, u32[]{:S(2)}) collective-permute-start(bf16[256,256]{1,0:T(8,128)(2,1)S(1)} %get-tuple-element.65), channel_id=1, source_target_pairs={{0,16},{16,0},{32,48},{48,32},{64,80},{80,64},{96,112},{112,96},{1... | collective-permute-start | bytes 393224 | tf_op jit(solution)/shard_map/ppermute | solution.py:283
  29.8 13.1 %collective-permute-start.4 = (bf16[256,256]{1,0:T(8,128)(2,1)S(1)}, bf16[256,256]{1,0:T(8,128)(2,1)S(1)}, u32[]{:S(2)}, u32[]{:S(2)}) collective-permute-start(bf16[256,256]{1,0:T(8,128)(2,1)S(1)} %get-tuple-element.66), channel_id=1, source_target_pairs={{0,1},{1,0},{2,3},{3,2},{4,5},{5,4},{6,7},{7,6},{8,9},{9,8},{10,11... | collective-permute-start | bytes 393224 | tf_op jit(solution)/shard_map/ppermute | solution.py:284
  34.0 24.7 %collective-permute-start.1 = (f32[256,128]{1,0:T(8,128)S(1)}, f32[256,128]{1,0:T(8,128)S(1)}, u32[]{:S(2)}, u32[]{:S(2)}) collective-permute-start(f32[256,128]{1,0:T(8,128)S(1)} %get-tuple-element.61.own_ref), channel_id=1, source_target_pairs={{0,16},{16,32},{32,48},{48,64},{64,80},{80,96},{96,112},{112,128},... | collective-permute-start | bytes 393224 | tf_op jit(solution)/shard_map/ppermute | solution.py:281
  37.7 21.1 %collective-permute-start.5 = (f32[256,128]{1,0:T(8,128)S(1)}, f32[256,128]{1,0:T(8,128)S(1)}, u32[]{:S(2)}, u32[]{:S(2)}) collective-permute-start(f32[256,128]{1,0:T(8,128)S(1)} %get-tuple-element.62.second_ref), channel_id=1, source_target_pairs={{0,1},{1,2},{2,3},{3,4},{4,5},{5,6},{6,7},{7,8},{8,9},{9,10},{10,1... | collective-permute-start | bytes 393224 | tf_op jit(solution)/shard_map/ppermute | solution.py:285
  40.5 1.0 copy-start.2
  42.2 50.3 %copy-start.10 = (bf16[256,512]{1,0:T(8,128)(2,1)S(1)}, bf16[256,512]{1,0:T(8,128)(2,1)}, u32[]{:S(2)}) copy-start(bf16[256,512]{1,0:T(8,128)(2,1)} %coarse_ref.3) | copy-start | bytes 786436
  58.7 1.0 copy-start.3
  66.7 42.5 %copy-start = (bf16[1,1,1024,1024]{3,2,1,0:T(8,128)(2,1)S(1)}, bf16[1,1,1024,1024]{3,2,1,0:T(8,128)(2,1)}, u32[]{:S(2)}) copy-start(bf16[1,1,1024,1024]{3,2,1,0:T(8,128)(2,1)} %param.7) | copy-start | bytes 6291460
  67.9 42.6 %copy-start.8 = (f32[1024,128]{1,0:T(8,128)}, f32[1024,128]{1,0:T(8,128)S(1)}, u32[]{:S(2)}) copy-start(f32[1024,128]{1,0:T(8,128)S(1)} %get-tuple-element.75.residual_ref.last_ref) | copy-start | bytes 1572868
  92.5 40.0 %copy-start.4 = (bf16[1,1,4,256,256]{4,3,2,1,0:T(8,128)(2,1)S(1)}, bf16[1,1,4,256,256]{4,3,2,1,0:T(8,128)(2,1)}, u32[]{:S(2)}) copy-start(bf16[1,1,4,256,256]{4,3,2,1,0:T(8,128)(2,1)} %param.6) | copy-start | bytes 1572868
  110.5 22.0 %collective-permute-start.6 = (f32[256,128]{1,0:T(8,128)S(1)}, f32[256,128]{1,0:T(8,128)S(1)}, u32[]{:S(2)}, u32[]{:S(2)}) collective-permute-start(f32[256,128]{1,0:T(8,128)S(1)} %get-tuple-element.79), channel_id=1, source_target_pairs={{0,496},{16,32},{32,16},{48,64},{64,48},{80,96},{96,80},{112,128},... | collective-permute-start | bytes 393224 | tf_op jit(solution)/shard_map/ppermute | solution.py:256
  115.1 17.4 %collective-permute-start.7 = (f32[256,128]{1,0:T(8,128)S(1)}, f32[256,128]{1,0:T(8,128)S(1)}, u32[]{:S(2)}, u32[]{:S(2)}) collective-permute-start(f32[256,128]{1,0:T(8,128)S(1)} %get-tuple-element.80), channel_id=1, source_target_pairs={{0,15},{1,2},{2,1},{3,4},{4,3},{5,6},{6,5},{7,8},{8,7},{9,10},{10,... | collective-permute-start | bytes 393224 | tf_op jit(solution)/shard_map/ppermute | solution.py:257
  117.0 15.5 %collective-permute-start.8 = (f32[256,128]{1,0:T(8,128)S(1)}, f32[256,128]{1,0:T(8,128)S(1)}, u32[]{:S(2)}, u32[]{:S(2)}) collective-permute-start(f32[256,128]{1,0:T(8,128)S(1)} %get-tuple-element.81), channel_id=1, source_target_pairs={{0,16},{16,0},{32,48},{48,32},{64,80},{80,64},{96,112},{112,96},{1... | collective-permute-start | bytes 393224 | tf_op jit(solution)/shard_map/ppermute | solution.py:258
  118.9 13.6 %collective-permute-start.9 = (f32[256,128]{1,0:T(8,128)S(1)}, f32[256,128]{1,0:T(8,128)S(1)}, u32[]{:S(2)}, u32[]{:S(2)}) collective-permute-start(f32[256,128]{1,0:T(8,128)S(1)} %get-tuple-element.82), channel_id=1, source_target_pairs={{0,1},{1,0},{2,3},{3,2},{4,5},{5,4},{6,7},{7,6},{8,9},{9,8},{10,11... | collective-permute-start | bytes 393224 | tf_op jit(solution)/shard_map/ppermute | solution.py:259
  139.7 32.0 %all-to-all-start.2 = ((f32[32,2,128]{2,1,0:T(2,128)}), f32[32,2,128]{2,1,0:T(2,128)S(1)}, u32[]{:S(2)}, u32[]{:S(2)}) async-start(f32[32,2,128]{2,1,0:T(2,128)} %get-tuple-element.83), calls=%async_computation.2 | async-start | bytes 65536 | tf_op jit(solution)/shard_map/all_to_all | solution.py:264
  151.6 26.5 %collective-permute-start.10 = (f32[256,128]{1,0:T(8,128)}, f32[256,128]{1,0:T(8,128)}, u32[]{:S(2)}, u32[]{:S(2)}) collective-permute-start(f32[256,128]{1,0:T(8,128)} %copy-done.18), channel_id=1, source_target_pairs={{0,496},{16,32},{32,16},{48,64},{64,48},{80,96},{96,80},{112,128},... | collective-permute-start | bytes 393224 | tf_op jit(solution)/shard_map/ppermute | solution.py:256
  165.1 15.6 %collective-permute-start.11 = (f32[256,128]{1,0:T(8,128)}, f32[256,128]{1,0:T(8,128)}, u32[]{:S(2)}, u32[]{:S(2)}) collective-permute-start(f32[256,128]{1,0:T(8,128)} %copy-done.17), channel_id=1, source_target_pairs={{0,15},{1,2},{2,1},{3,4},{4,3},{5,6},{6,5},{7,8},{8,7},{9,10},{10,... | collective-permute-start | bytes 393224 | tf_op jit(solution)/shard_map/ppermute | solution.py:257
  167.8 12.8 %collective-permute-start.12 = (f32[256,128]{1,0:T(8,128)}, f32[256,128]{1,0:T(8,128)}, u32[]{:S(2)}, u32[]{:S(2)}) collective-permute-start(f32[256,128]{1,0:T(8,128)} %copy-done.16), channel_id=1, source_target_pairs={{0,16},{16,0},{32,48},{48,32},{64,80},{80,64},{96,112},{112,96},{1... | collective-permute-start | bytes 393224 | tf_op jit(solution)/shard_map/ppermute | solution.py:258
  169.8 10.9 %collective-permute-start.13 = (f32[256,128]{1,0:T(8,128)}, f32[256,128]{1,0:T(8,128)}, u32[]{:S(2)}, u32[]{:S(2)}) collective-permute-start(f32[256,128]{1,0:T(8,128)} %copy-done.15), channel_id=1, source_target_pairs={{0,1},{1,0},{2,3},{3,2},{4,5},{5,4},{6,7},{7,6},{8,9},{9,8},{10,11... | collective-permute-start | bytes 393224 | tf_op jit(solution)/shard_map/ppermute | solution.py:259
  172.3 12.0 %all-to-all-start.3 = ((f32[16,2,128]{2,1,0:T(2,128)}), f32[16,2,128]{2,1,0:T(2,128)S(1)}, u32[]{:S(2)}, u32[]{:S(2)}) async-start(f32[16,2,128]{2,1,0:T(2,128)} %sum.3), calls=%async_computation.3 | async-start | bytes 32768 | tf_op jit(solution)/shard_map/all_to_all | solution.py:266
  184.4 1.0 copy-start.9
  215.8 67.2 %copy-start.5 = (bf16[1,1,4,256,256]{4,3,2,1,0:T(8,128)(2,1)S(1)}, bf16[1,1,4,256,256]{4,3,2,1,0:T(8,128)(2,1)}, u32[]{:S(2)}) copy-start(bf16[1,1,4,256,256]{4,3,2,1,0:T(8,128)(2,1)} %param.6) | copy-start | bytes 1572868
  215.8 67.2 %copy-start.7 = (f32[1024,128]{1,0:T(8,128)S(1)}, f32[1024,128]{1,0:T(8,128)}, u32[]{:S(2)}) copy-start(f32[1024,128]{1,0:T(8,128)} %copy-done.6) | copy-start | bytes 1572868
  234.8 48.2 %collective-permute-start.14 = (f32[256,128]{1,0:T(8,128)S(1)}, f32[256,128]{1,0:T(8,128)S(1)}, u32[]{:S(2)}, u32[]{:S(2)}) collective-permute-start(f32[256,128]{1,0:T(8,128)S(1)} %get-tuple-element.99), channel_id=1, source_target_pairs={{0,496},{16,32},{32,16},{48,64},{64,48},{80,96},{96,80},{112,128},... | collective-permute-start | bytes 393224 | tf_op jit(solution)/shard_map/ppermute | solution.py:256
  238.6 44.4 %collective-permute-start.15 = (f32[256,128]{1,0:T(8,128)S(1)}, f32[256,128]{1,0:T(8,128)S(1)}, u32[]{:S(2)}, u32[]{:S(2)}) collective-permute-start(f32[256,128]{1,0:T(8,128)S(1)} %get-tuple-element.100), channel_id=1, source_target_pairs={{0,15},{1,2},{2,1},{3,4},{4,3},{5,6},{6,5},{7,8},{8,7},{9,10},{10,... | collective-permute-start | bytes 393224 | tf_op jit(solution)/shard_map/ppermute | solution.py:257
  240.5 42.5 %collective-permute-start.16 = (f32[256,128]{1,0:T(8,128)S(1)}, f32[256,128]{1,0:T(8,128)S(1)}, u32[]{:S(2)}, u32[]{:S(2)}) collective-permute-start(f32[256,128]{1,0:T(8,128)S(1)} %get-tuple-element.101), channel_id=1, source_target_pairs={{0,16},{16,0},{32,48},{48,32},{64,80},{80,64},{96,112},{112,96},{1... | collective-permute-start | bytes 393224 | tf_op jit(solution)/shard_map/ppermute | solution.py:258
  242.4 40.6 %collective-permute-start.17 = (f32[256,128]{1,0:T(8,128)S(1)}, f32[256,128]{1,0:T(8,128)S(1)}, u32[]{:S(2)}, u32[]{:S(2)}) collective-permute-start(f32[256,128]{1,0:T(8,128)S(1)} %get-tuple-element.102), channel_id=1, source_target_pairs={{0,1},{1,0},{2,3},{3,2},{4,5},{5,4},{6,7},{7,6},{8,9},{9,8},{10,11... | collective-permute-start | bytes 393224 | tf_op jit(solution)/shard_map/ppermute | solution.py:259
  285.4 40.3 %collective-permute-start.18 = (f32[256,128]{1,0:T(8,128)S(1)}, f32[256,128]{1,0:T(8,128)S(1)}, u32[]{:S(2)}, u32[]{:S(2)}) collective-permute-start(f32[256,128]{1,0:T(8,128)S(1)} %get-tuple-element.111), channel_id=1, source_target_pairs={{0,496},{16,0},{32,16},{48,32},{64,48},{80,64},{96,80},{112,96},{1... | collective-permute-start | bytes 393224 | tf_op jit(solution)/shard_map/ppermute | solution.py:332
  289.0 36.6 %collective-permute-start.19 = (f32[256,128]{1,0:T(8,128)S(1)}, f32[256,128]{1,0:T(8,128)S(1)}, u32[]{:S(2)}, u32[]{:S(2)}) collective-permute-start(f32[256,128]{1,0:T(8,128)S(1)} %get-tuple-element.112), channel_id=1, source_target_pairs={{0,15},{1,0},{2,1},{3,2},{4,3},{5,4},{6,5},{7,6},{8,7},{9,8},{10,9... | collective-permute-start | bytes 393224 | tf_op jit(solution)/shard_map/ppermute | solution.py:333
  (9 other events, 6.9 us)

commit v2 on v1

--- a/solution.py
+++ b/solution.py
@@ -15,8 +15,8 @@
 COLUMN = ("zh", "zl", "core")
 PLANE = ("y", "x")
 HIGHEST = lax.Precision.HIGHEST
-ROUGH_STEPS = 12
-FINE_STEPS = 64
+ROUGH_STEPS = 6
+FINE_STEPS = 32
 VMEM = pl.BlockSpec(memory_space=pltpu.VMEM)
 SMEM = pl.BlockSpec(memory_space=pltpu.SMEM)
 
@@ -66,20 +66,59 @@
     return slice(number * F, (number + 1) * F)
 
 
-def prepare_kernel(even_ref, rhs_ref, blocks_ref, slab_b, first_ref, patch_b, slab_a, patch_a, second_ref):
-    for even, ahead, back, a_ref, b_ref in ((even_ref[0], 0, 2, slab_a, slab_b), (even_ref[1], 1, 3, patch_a, patch_b)):
-        @pl.when(even == 1)
-        def _():
-            b_ref[...] = blocks_ref[back]
-            a_ref[...] = blocks_ref[ahead]
-
-        @pl.when(even == 0)
-        def _():
-            b_ref[...] = blocks_ref[ahead]
-            a_ref[...] = blocks_ref[back]
-
+HALF = F // 2
+PAD = 16
+PACKED = F + PAD
+
+
+def square_masks():
+    row = lax.broadcasted_iota(jnp.int32, (HALF, HALF), 0)
+    column = lax.broadcasted_iota(jnp.int32, (HALF, HALF), 1)
+    return row > column, row == column, row < column
+
+
+def turn_kernel(rhs_ref, first_ref, second_ref):
     first_ref[...] = rhs_ref[:, 0, :].T
     second_ref[...] = rhs_ref[:, 1, :].T
+
+
+def pack_kernel(even_ref, second_ref, blocks_ref, slab_b, patch_b, slab_a, patch_a):
+    lower, diagonal, upper = square_masks()
+    for f in range(4):
+        b_ref, a_ref = ((slab_b, slab_a), (patch_b, patch_a))[f % 2]
+        use_a = even_ref[f % 2] == (1 if f < 2 else 0)
+
+        def pack(out_ref):
+            kind = out_ref.dtype
+            block = blocks_ref[f].astype(jnp.float32)
+            first, second = block[:HALF, :HALF], block[HALF:, HALF:]
+            out_ref[:HALF] = jnp.where(upper, second, first).astype(kind)
+            out_ref[HALF:F] = block[HALF:, :HALF].astype(kind)
+            row = jnp.sum(jnp.where(diagonal, second, 0.0), axis=0, keepdims=True)
+            out_ref[F:PACKED] = jnp.broadcast_to(row, (PAD, HALF)).astype(kind)
+            if f % 2:
+                out_ref[PACKED:] = second_ref[...]
+
+        @pl.when(use_a)
+        def _():
+            pack(a_ref)
+
+        @pl.when(jnp.logical_not(use_a))
+        def _():
+            pack(b_ref)
+
+
+def unpack(part_ref, out_ref):
+    lower, diagonal, upper = square_masks()
+    mixed, below = part_ref[:HALF].astype(jnp.float32), part_ref[HALF:F].astype(jnp.float32)
+    corner = part_ref[F:PACKED].astype(jnp.float32)[:1]
+    first = jnp.where(upper, 0.0, mixed)
+    second = jnp.where(upper, mixed, 0.0)
+    out_ref[:HALF, :HALF] = out_ref[:HALF, :HALF] + (first + jnp.where(lower, first, 0.0).T)
+    out_ref[HALF:, HALF:] = out_ref[HALF:, HALF:] + (
+        second + second.T + jnp.where(diagonal, corner, 0.0))
+    out_ref[HALF:, :HALF] = out_ref[HALF:, :HALF] + below
+    out_ref[:HALF, HALF:] = out_ref[:HALF, HALF:] + below.T
 
 
 def primal_kernel(ids_ref, blocks_ref, primal_ref):
@@ -92,26 +131,64 @@
         primal_ref[:, rows(f)] = rough_dot(onehot[:, rows(f)], blocks_ref[f]).astype(jnp.bfloat16)
 
 
-def invert_kernel(even_ref, blocks_ref, slab_b, patch_b, slab_a, patch_a, out_ref, a_ref):
+def invert_kernel(flag, even_ref, part_b, part_a, blocks_ref, right_ref, shared_ref, factors_ref, residual_ref,
+                  lifted_ref, a_ref):
+    for k in range(2):
+        use_a = even_ref[flag] == 1 - k
+        a_ref[k] = blocks_ref[2 * k + flag].astype(jnp.float32)
+
+        def take(part_ref):
+            unpack(part_ref, a_ref.at[k])
+            if k == 1 and flag == 1:
+                residual_ref[rows(1)] = part_ref[PACKED:]
+
+        @pl.when(use_a)
+        def _():
+            take(part_a)
+
+        @pl.when(jnp.logical_not(use_a))
+        def _():
+            take(part_b)
+
+    residual_ref[rows(0)] = right_ref[...]
+    if flag == 0:
+        residual_ref[rows(1)] = shared_ref[...]
+    invert(factors_ref, a_ref)
+    for k in range(2):
+        lifted_ref[rows(k)] = fine_dot(factors_ref[k], residual_ref[rows(k)])
+
+
+def begin_kernel(even_ref, from_slab, slab_b, slab_a, blocks_ref, first_ref, primal_ref, patch_residual_ref,
+                 patch_lifted_ref, factors_ref, residual_ref, lifted_ref, rounded_ref, c_ref, a_ref, some_ref, solved_ref):
+    invert_kernel(0, even_ref, slab_b, slab_a, blocks_ref, first_ref, from_slab, factors_ref, some_ref, solved_ref, a_ref)
+    for k in range(2):
+        for flag, part, solved in ((0, some_ref, solved_ref), (1, patch_residual_ref, patch_lifted_ref)):
+            residual_ref[rows(2 * k + flag)] = part[rows(k)]
+            lifted_ref[rows(2 * k + flag)] = solved[rows(k)]
+    rounded_ref[...] = lifted_ref[...].astype(jnp.bfloat16)
+    restrict(primal_ref, rounded_ref, c_ref)
+
+
+def invert(out_ref, a_ref):
     index = lax.broadcasted_iota(jnp.int32, (F, F), 0)
     unit = (index == lax.broadcasted_iota(jnp.int32, (F, F), 1)).astype(jnp.float32)
 
-    def start(f):
-        bound = jnp.max(jnp.sum(jnp.abs(a_ref[f]), axis=0, keepdims=True), axis=1, keepdims=True)
-        return unit * (1.9 / bound)
-
-    for f in range(4):
-        b, a = ((slab_b, slab_a), (patch_b, patch_a))[f % 2]
-        other = jnp.where(even_ref[f % 2] == (1 if f < 2 else 0), a[...], b[...])
-        a_ref[f] = blocks_ref[f].astype(jnp.float32) + other.astype(jnp.float32)
-        out_ref[f] = start(f)
+    def start(f, safe):
+        diagonal = jnp.sum(unit * a_ref[f], axis=0, keepdims=True)
+        if not safe:
+            return unit / diagonal
+        ratio = jnp.sum(jnp.abs(a_ref[f]), axis=0, keepdims=True) / diagonal
+        return unit * (1.9 / (jnp.max(ratio, axis=1, keepdims=True) * diagonal))
+
+    for f in range(2):
+        out_ref[f] = start(f, False)
 
     def newton(multiply):
-        lefts = [unit - multiply(a_ref[f], out_ref[f]) for f in range(4)]
+        lefts = [unit - multiply(a_ref[f], out_ref[f]) for f in range(2)]
         worst = jnp.float32(0.0)
-        for f in range(4):
+        for f in range(2):
             worst = jnp.maximum(worst, jnp.sum(lefts[f] * lefts[f]))
-        for f in range(4):
+        for f in range(2):
             out_ref[f] = out_ref[f] + multiply(out_ref[f], lefts[f])
         return worst
 
@@ -120,40 +197,37 @@
 
     def rough_body(carry):
         step, _ = carry
+        newton(rough)
         return step + 1, newton(rough)
 
-    _, worst = lax.while_loop(lambda c: (c[0] < ROUGH_STEPS) & ~(c[1] < 0.25), rough_body, (0, jnp.float32(1e30)))
-
-    @pl.when(~(worst < 0.25))
+    lax.while_loop(lambda c: (c[0] < ROUGH_STEPS) & ~(c[1] < 0.25), rough_body, (0, jnp.float32(1e30)))
+
+    good = newton(fine_dot) < 0.5
+    worst = jnp.where(good, newton(fine_dot), 1e30)
+
+    @pl.when(jnp.logical_not(good))
     def _():
-        for f in range(4):
-            out_ref[f] = start(f)
+        for f in range(2):
+            out_ref[f] = start(f, True)
 
     def fine_body(carry):
         step, last, _ = carry
+        newton(fine_dot)
         return step + 1, newton(fine_dot), last
 
     lax.while_loop(
         lambda c: (c[0] < FINE_STEPS) & (c[1] > 1e-6) & ~((c[1] < 1e-2) & (c[1] >= c[2])),
-        fine_body, (0, jnp.float32(1e30), jnp.float32(1e31)))
-
-
-def solve_and_restrict(residual_of, factors_ref, primal_ref, lifted_ref, rounded_ref, c_ref):
-    for f in range(4):
-        lifted = fine_dot(factors_ref[f], residual_of(f))
-        lifted_ref[rows(f)] = lifted
-        rounded_ref[rows(f)] = lifted.astype(jnp.bfloat16)
+        fine_body, (0, worst, jnp.float32(1e31)))
+
+
+def restrict(primal_ref, rounded_ref, c_ref):
     c = rough_dot(primal_ref[...], rounded_ref[...]).astype(jnp.bfloat16)
     for j in range(32):
         c_ref[j] = c
 
 
-def first_kernel(own_ref, second_ref, slab_ref, patch_ref, factors_ref, primal_ref, residual_ref, lifted_ref, rounded_ref, c_ref):
-    residual_ref[rows(0)] = own_ref[...]
-    residual_ref[rows(1)] = second_ref[...]
-    residual_ref[rows(2)] = slab_ref[...]
-    residual_ref[rows(3)] = patch_ref[...]
-    solve_and_restrict(lambda f: residual_ref[rows(f)], factors_ref, primal_ref, lifted_ref, rounded_ref, c_ref)
+def factor(factor_refs, f):
+    return factor_refs[f % 2][f // 2]
 
 
 def write_parts(even_ref, terms_ref, outs):
@@ -206,11 +280,11 @@
         scale = jnp.sum(sums_ref[...], axis=0) / jnp.sum(before_ref[...], axis=0)[:1]
     else:
         over_ref, *refs = refs
-    (even_ref, terms_ref, slab_b, patch_b, slab_a, patch_a, lifted_ref, factors_ref, blocks_ref, inverse_ref,
+    (even_ref, terms_ref, slab_b, patch_b, slab_a, patch_a, lifted_ref, slab_factors, patch_factors, blocks_ref, inverse_ref,
      direction_ref, image_ref, product_ref, *outs, rounded_ref) = refs
     got = (slab_b, patch_b, slab_a, patch_a)
     for f in range(4):
-        value = lifted_ref[rows(f)] + fine_dot(factors_ref[f], assembled(even_ref, terms_ref, got, f))
+        value = lifted_ref[rows(f)] + fine_dot(factor((slab_factors, patch_factors), f), assembled(even_ref, terms_ref, got, f))
         if again:
             value = value + scale * last_ref[rows(f)]
         direction_ref[rows(f)] = value
@@ -228,14 +302,17 @@
         write_parts(even_ref, image_ref, outs)
 
 
-def update_kernel(even_ref, sums_ref, image_ref, slab_b, patch_b, slab_a, patch_a, last_ref, factors_ref, primal_ref,
-                  residual_ref, lifted_ref, rounded_ref, c_ref):
+def update_kernel(even_ref, sums_ref, image_ref, slab_b, patch_b, slab_a, patch_a, last_ref, slab_factors,
+                  patch_factors, primal_ref, residual_ref, lifted_ref, rounded_ref, c_ref):
     sums = jnp.sum(sums_ref[...], axis=0)
     step = sums[:1] / sums[1:]
     got = (slab_b, patch_b, slab_a, patch_a)
     for f in range(4):
         residual_ref[rows(f)] = last_ref[rows(f)] - step * assembled(even_ref, image_ref, got, f)
-    solve_and_restrict(lambda f: residual_ref[rows(f)], factors_ref, primal_ref, lifted_ref, rounded_ref, c_ref)
+        lifted = fine_dot(factor((slab_factors, patch_factors), f), residual_ref[rows(f)])
+        lifted_ref[rows(f)] = lifted
+        rounded_ref[rows(f)] = lifted.astype(jnp.bfloat16)
+    restrict(primal_ref, rounded_ref, c_ref)
 
 
 def last_kernel(first_ref, over_ref, under_ref, first_direction_ref, direction_ref, residual_ref, image_ref,
@@ -274,23 +351,12 @@
     patch_even = 1 - lax.axis_index("core")
     even = jnp.stack([slab_even, patch_even]).astype(jnp.int32)
 
-    slab_b, first, patch_b, slab_a, patch_a, second = call(
-        prepare_kernel, [bf16(F, F), f32(F, RHS)] + [bf16(F, F)] * 3 + [f32(F, RHS)], [SMEM, VMEM, VMEM], "prepare")(
-            even, rhs[0, 0], blocks)
-    slab_b = lax.ppermute(slab_b, SLAB, even_pairs(32))
+    first, second = call(turn_kernel, [f32(F, RHS)] * 2, [VMEM], "turn")(rhs[0, 0])
     from_slab = lax.ppermute(first, SLAB, roll_pairs(32, 1))
-    patch_b = lax.ppermute(patch_b, PATCH, even_pairs(16))
-    slab_a = lax.ppermute(slab_a, SLAB, odd_pairs(32))
-    patch_a = lax.ppermute(patch_a, PATCH, odd_pairs(16))
-    from_patch = lax.ppermute(second, PATCH, roll_pairs(16, 1))
+    send = call(
+        pack_kernel, [bf16(PACKED, HALF), f32(PACKED + F, HALF)] * 2, [SMEM, VMEM, VMEM], "pack")(even, second, blocks)
+    got = swap(send)
     primal = call(primal_kernel, bf16(PRIM, NI), [SMEM, VMEM], "primal")(ids, blocks)
-    slab_b, from_slab, patch_b, slab_a, patch_a, from_patch = lax.optimization_barrier(
-        (slab_b, from_slab, patch_b, slab_a, patch_a, from_patch))
-    got = (slab_b, patch_b, slab_a, patch_a)
-
-    factors = call(invert_kernel, f32(4, F, F), [SMEM] + [VMEM] * 5, "invert", 4 * 16 * 2 * F ** 3,
-                   [pltpu.VMEM((4, F, F), jnp.float32)])(even, blocks, *got)
-
     field = f32(NI, RHS)
     part = [f32(F, RHS)] * 4
     solved = [field, field, bf16(NI, RHS), bf16(32, PRIM, RHS)]
@@ -306,33 +372,39 @@
         return terms, product, send
 
     scratch = [pltpu.VMEM((NI, RHS), jnp.bfloat16)]
-    residual, lifted, rounded, c = call(first_kernel, solved, [VMEM] * 6, "first", solve_flops)(
-        first, second, from_slab, from_patch, factors, primal)
+    pair = [f32(2, F, F), f32(2 * F, RHS), f32(2 * F, RHS)]
+    square = pltpu.VMEM((2, F, F), jnp.float32)
+    patch_factors, patch_residual, patch_lifted = call(
+        lambda even_ref, part_b, part_a, blocks_ref, right_ref, *refs: invert_kernel(
+            1, even_ref, part_b, part_a, blocks_ref, right_ref, None, *refs),
+        pair, [SMEM] + [VMEM] * 4, "invert", 1 << 32, [square])(even, got[1], got[3], blocks, second)
+    slab_factors, residual, lifted, rounded, c = call(
+        begin_kernel, pair[:1] + solved, [SMEM] + [VMEM] * 8, "begin", 1 << 32,
+        [square, pltpu.VMEM((2 * F, RHS), jnp.float32), pltpu.VMEM((2 * F, RHS), jnp.float32)])(
+            even, from_slab, got[0], got[2], blocks, first, primal, patch_residual, patch_lifted)
+    factors = (slab_factors, patch_factors)
     terms, product, send = coarse_terms(residual, lifted, rounded, c)
     got = swap(send)
     first_direction, image, spread, *send = call(
         lambda *refs: direction_kernel(False, *refs), [field, field, f32(32, 2, RHS)] + part,
-        [VMEM, SMEM] + [VMEM] * 9, "direction", solve_flops, scratch)(
-            product, even, terms, *got, lifted, factors, blocks, inverse)
+        [VMEM, SMEM] + [VMEM] * 10, "direction", solve_flops, scratch)(
+            product, even, terms, *got, lifted, *factors, blocks, inverse)
 
     got = swap(send)
     first_sums = total_parts(spread)
-    first_sums, got = lax.optimization_barrier((first_sums, got))
-    residual, lifted, rounded, c = call(update_kernel, solved, [SMEM] + [VMEM] * 9, "update", solve_flops)(
-        even, first_sums, image, *got, residual, factors, primal)
+    residual, lifted, rounded, c = call(update_kernel, solved, [SMEM] + [VMEM] * 10, "update", solve_flops)(
+        even, first_sums, image, *got, residual, *factors, primal)
     terms, spread, send = coarse_terms(residual, lifted, rounded, c)
     got = swap(send)
     over = total_parts(spread)
-    over, got = lax.optimization_barrier((over, got))
     direction, image, spread, *send = call(
         lambda *refs: direction_kernel(True, *refs), [field, field, f32(32, 1, RHS)] + part[:2],
-        [VMEM] * 3 + [SMEM] + [VMEM] * 9, "direction_again", solve_flops, scratch)(
-            over, first_sums, first_direction, even, terms, *got, lifted, factors, blocks, inverse)
+        [VMEM] * 3 + [SMEM] + [VMEM] * 10, "direction_again", solve_flops, scratch)(
+            over, first_sums, first_direction, even, terms, *got, lifted, *factors, blocks, inverse)
 
     from_slab = lax.ppermute(send[0], SLAB, roll_pairs(32, -1))
     from_patch = lax.ppermute(send[1], PATCH, roll_pairs(16, -1))
     under = total_parts(spread)
-    under, from_slab, from_patch = lax.optimization_barrier((under, from_slab, from_patch))
     solution, residual = call(last_kernel, [f32(RHS, 2, F)] * 2, [VMEM] * 9, "last")(
         first_sums, over, under, first_direction, direction, residual, image, from_slab, from_patch)
     return (solution.reshape(1, 1, RHS, 2, F), residual.reshape(1, 1, RHS, 2, F))

time: 328 us -> 320 us (0.976)
  waiting for transfers between devices: 30.5 us -> 21.7 us
    ppermute x5 -> x0, starting transfers between devices: 33.3 us -> none  [the longest x1 20.9 us: on_device(): slab_b = lax.ppermute(slab_b, SLAB, even_pairs(32))]
    ppermute x3 -> x4, starting transfers between devices: 21.9 us -> 39.3 us  [swap(): lax.ppermute(slab_b, SLAB, even_pairs(32))]
    ppermute x1, waiting for transfers between devices: 15.8 us -> 0.01 us  [on_device(): from_slab = lax.ppermute(first, SLAB, roll_pairs(32, 1))]
    ppermute x3 -> x4, starting transfers between devices: 12.4 us -> 23.5 us  [swap(): lax.ppermute(patch_a, PATCH, odd_pairs(16))]
    ppermute x3 -> x4, waiting for transfers between devices: 8.35 us -> 15.4 us  [swap(): lax.ppermute(slab_b, SLAB, even_pairs(32))]
    ppermute x3 -> x4, starting transfers between devices: 6.56 us -> 11.5 us  [swap(): lax.ppermute(patch_b, PATCH, even_pairs(16))]
    all_to_all x1, starting transfers between devices: 11.9 us -> 8.04 us  [total_parts(): parts = lax.all_to_all(spread, COLUMN, 0, 0)]
    pallas_call x4 -> x5, Pallas kernels: 11.2 us -> 13.3 us  [the longest x1 5.22 us: on_device(): call(begin_kernel, pair[:1] + solved, [SMEM] + [VMEM] * 8, 'begin', 1 <<...]
  transfers between devices with their start and end apart: 22 -> 21, of which waited for: 4 -> 4; matrix products, arithmetic and copies ran while one was open for 0% -> 0% of each run, Pallas kernels for 0% -> 2%
where the time goes in v2:
time: 320 us; the launch traced here: 319 us
  blocking collectives  154 us (48%)
  starting transfers between devices  106 us (33%)
  Pallas kernels  24.2 us (8%)
  waiting for transfers between devices  21.7 us (7%)
  local copies, waits for them, and re-layouts  12 us (4%)
    all_to_all x2, blocking collectives, coarse_terms(): gathered = lax.all_to_all(c, SLAB, 0, 0)  50.6 us
    all_to_all x2, blocking collectives, total_parts(): parts = lax.all_to_all(spread, COLUMN, 0, 0)  46.6 us
    ppermute x4, starting transfers between devices, swap(): lax.ppermute(slab_b, SLAB, even_pairs(32))  39.3 us
    all_to_all x2, blocking collectives, coarse_terms(): parts = lax.all_to_all(partial, PATCH, 0, 0)  36.1 us
    ppermute x4, starting transfers between devices, swap(): lax.ppermute(patch_a, PATCH, odd_pairs(16))  23.5 us
    all_to_all x2, blocking collectives, total_parts(): return lax.all_to_all(spread, PLANE, 0, 0)  20.9 us
    ppermute x4, waiting for transfers between devices, swap(): lax.ppermute(slab_b, SLAB, even_pairs(32))  15.4 us
    unnamed x42, local copies, waits for them, and re-layouts  12 us
  transfers between devices with their start and end apart: 21, of which 4 were waited for; matrix products, arithmetic and copies ran while one was open for 0% of the time, Pallas kernels for 2%

profile of v2, /device:TPU:1, one launch (start us, length us, event | category | flops | bytes accessed | tf_op | source)
XLA Modules:
  0.0 318.9 jit_solution(10656144212308498370)
XLA Ops:
  3.5 4.9 %collective-permute-start.3 = (f32[528,128]{1,0:T(8,128)S(1)}, f32[528,128]{1,0:T(8,128)S(1)}, u32[]{:S(2)}, u32[]{:S(2)}) collective-permute-start(f32[528,128]{1,0:T(8,128)S(1)} %get-tuple-element.50), channel_id=1, source_target_pairs={{0,15},{1,2},{2,1},{3,4},{4,3},{5,6},{6,5},{7,8},{8,7},{9,10},{10,... | collective-permute-start | bytes 811016 | tf_op jit(solution)/shard_map/ppermute | solution.py:334
  8.5 11.1 %collective-permute-start.4 = (f32[528,128]{1,0:T(8,128)S(1)}, f32[528,128]{1,0:T(8,128)S(1)}, u32[]{:S(2)}, u32[]{:S(2)}) collective-permute-start(f32[528,128]{1,0:T(8,128)S(1)} %get-tuple-element.51), channel_id=1, source_target_pairs={{0,1},{1,0},{2,3},{3,2},{4,5},{5,4},{6,7},{7,6},{8,9},{9,8},{10,11... | collective-permute-start | bytes 811016 | tf_op jit(solution)/shard_map/ppermute | solution.py:336
  19.6 3.1 collective-permute-start
  22.7 15.1 %collective-permute-start.1 = (bf16[272,128]{1,0:T(8,128)(2,1)S(1)}, bf16[272,128]{1,0:T(8,128)(2,1)S(1)}, u32[]{:S(2)}, u32[]{:S(2)}) collective-permute-start(bf16[272,128]{1,0:T(8,128)(2,1)S(1)} %get-tuple-element.48), channel_id=1, source_target_pairs={{0,496},{16,32},{32,16},{48,64},{64,48},{80,96},{96,80},{112,128},... | collective-permute-start | bytes 208904 | tf_op jit(solution)/shard_map/ppermute | solution.py:333
  43.2 4.9 %invert.1 = (f32[2,256,256]{2,1,0:T(8,128)S(1)}, f32[512,128]{1,0:T(8,128)S(1)}, f32[512,128]{1,0:T(8,128)S(1)}) custom-call(s32[2]{0:T(128)S(1)} %pad_add_fusion.even_ref.refs_1_.refs_3_, f32[528,128]{1,0:T(8,128)S(1)} %collective-permute-done.3.part_b, f32[528,128]{1,0:T(8,128)S(1)} %collective-permute-done.4.part_a, bf16[4,256,256]{2,1,0:T(8,128)(2,1)S(1)} %bitcast.14, ...), custom_call_target="tpu_custom_call" | custom-call | flops 4294967296 | bytes 1048576 | tf_op jit(solution)/shard_map/invert/pallas_call | solution.py:377
  48.1 5.5 %collective-permute-done.1.slab_b = bf16[272,128]{1,0:T(8,128)(2,1)S(1)} collective-permute-done((bf16[272,128]{1,0:T(8,128)(2,1)S(1)}, bf16[272,128]{1,0:T(8,128)(2,1)S(1)}, u32[]{:S(2)}, u32[]{:S(2)}) %collective-permute-start.1) | collective-permute-done | bytes 69664 | tf_op jit(solution)/shard_map/ppermute | solution.py:333
  53.7 5.2 %begin.1 = (f32[2,256,256]{2,1,0:T(8,128)S(1)}, f32[1024,128]{1,0:T(8,128)S(1)}, f32[1024,128]{1,0:T(8,128)S(1)}, bf16[1024,128]{1,0:T(8,128)(2,1)S(1)}, bf16[32,16,128]{2,1,0:T(8,128)(2,1)S(1)}) custom-call(s32[2]{0:T(128)S(1)} %pad_add_fusion.even_ref.refs_1_.refs_3_, f32[256,128]{1,0:T(8,128)S(1)} %collective-permute-done.from_slab, ...), custom_call_target="tpu_custom_call" | custom-call | flops 4294967296 | bytes 1048576 | tf_op jit(solution)/shard_map/begin/pallas_call | solution.py:381
  58.9 23.6 %all_to_all.50.gathered_ref = bf16[32,16,128]{2,1,0:T(8,128)(2,1)S(1)} all-to-all(bf16[32,16,128]{2,1,0:T(8,128)(2,1)S(1)} %get-tuple-element.54), channel_id=1, replica_groups=mesh['zh'=2,'y'=4,'x'=4,'zl'=8,'core'=2] {'zh','y','x'}, dimensions={0} | all-to-all | bytes 262144 | tf_op jit(solution)/shard_map/all_to_all | solution.py:366
  82.8 18.0 %all_to_all.51.parts_ref = f32[16,16,128]{2,1,0:T(8,128)S(1)} all-to-all(f32[16,16,128]{2,1,0:T(8,128)S(1)} %coarse.2), channel_id=1, replica_groups=mesh['zh'=2,'y'=4,'x'=4,'zl'=8,'core'=2] {'zl','core'}, dimensions={0} | all-to-all | bytes 262144 | tf_op jit(solution)/shard_map/all_to_all | solution.py:368
  102.2 5.8 %collective-permute-start.5 = (f32[256,128]{1,0:T(8,128)S(1)}, f32[256,128]{1,0:T(8,128)S(1)}, u32[]{:S(2)}, u32[]{:S(2)}) collective-permute-start(f32[256,128]{1,0:T(8,128)S(1)} %get-tuple-element.60), channel_id=1, source_target_pairs={{0,496},{16,32},{32,16},{48,64},{64,48},{80,96},{96,80},{112,128},... | collective-permute-start | bytes 393224 | tf_op jit(solution)/shard_map/ppermute | solution.py:333
  111.8 5.2 %collective-permute-start.8 = (f32[256,128]{1,0:T(8,128)S(1)}, f32[256,128]{1,0:T(8,128)S(1)}, u32[]{:S(2)}, u32[]{:S(2)}) collective-permute-start(f32[256,128]{1,0:T(8,128)S(1)} %get-tuple-element.63), channel_id=1, source_target_pairs={{0,1},{1,0},{2,3},{3,2},{4,5},{5,4},{6,7},{7,6},{8,9},{9,8},{10,11... | collective-permute-start | bytes 393224 | tf_op jit(solution)/shard_map/ppermute | solution.py:336
  117.0 9.8 %collective-permute-done.5.refs_3_ = f32[256,128]{1,0:T(8,128)S(1)} collective-permute-done((f32[256,128]{1,0:T(8,128)S(1)}, f32[256,128]{1,0:T(8,128)S(1)}, u32[]{:S(2)}, u32[]{:S(2)}) %collective-permute-start.5) | collective-permute-done | bytes 131104 | tf_op jit(solution)/shard_map/ppermute | solution.py:333
  126.9 2.9 direction.1
  134.0 8.0 %all-to-all-start.2 = ((f32[32,2,128]{2,1,0:T(2,128)}), f32[32,2,128]{2,1,0:T(2,128)S(1)}, u32[]{:S(2)}, u32[]{:S(2)}) async-start(f32[32,2,128]{2,1,0:T(2,128)} %get-tuple-element.66), calls=%async_computation.2 | async-start | bytes 65536 | tf_op jit(solution)/shard_map/all_to_all | solution.py:341
  142.1 14.6 %collective-permute-start.9 = (f32[256,128]{1,0:T(8,128)}, f32[256,128]{1,0:T(8,128)}, u32[]{:S(2)}, u32[]{:S(2)}) collective-permute-start(f32[256,128]{1,0:T(8,128)} %copy-done.20), channel_id=1, source_target_pairs={{0,496},{16,32},{32,16},{48,64},{64,48},{80,96},{96,80},{112,128},... | collective-permute-start | bytes 393224 | tf_op jit(solution)/shard_map/ppermute | solution.py:333
  156.7 2.7 collective-permute-start.10
  159.4 1.9 collective-permute-start.11
  163.9 4.7 %all-to-all-start.3 = ((f32[16,2,128]{2,1,0:T(2,128)}), f32[16,2,128]{2,1,0:T(2,128)S(1)}, u32[]{:S(2)}, u32[]{:S(2)}) async-start(f32[16,2,128]{2,1,0:T(2,128)} %sum.3), calls=%async_computation.3 | async-start | bytes 32768 | tf_op jit(solution)/shard_map/all_to_all | solution.py:343
  168.6 3.6 %collective-permute-done.10.patch_b = f32[256,128]{1,0:T(8,128)} collective-permute-done((f32[256,128]{1,0:T(8,128)}, f32[256,128]{1,0:T(8,128)}, u32[]{:S(2)}, u32[]{:S(2)}) %collective-permute-start.10) | collective-permute-done | bytes 131104 | tf_op jit(solution)/shard_map/ppermute | solution.py:334
  172.2 2.6 all-to-all-done.3.sums_ref.refs_1_.first_ref
  178.0 2.4 update.1
  180.4 27.0 %all_to_all.52.gathered_ref = bf16[32,16,128]{2,1,0:T(8,128)(2,1)S(1)} all-to-all(bf16[32,16,128]{2,1,0:T(8,128)(2,1)S(1)} %get-tuple-element.72), channel_id=1, replica_groups=mesh['zh'=2,'y'=4,'x'=4,'zl'=8,'core'=2] {'zh','y','x'}, dimensions={0} | all-to-all | bytes 262144 | tf_op jit(solution)/shard_map/all_to_all | solution.py:366
  207.6 18.1 %all_to_all.53.parts_ref = f32[16,16,128]{2,1,0:T(8,128)S(1)} all-to-all(f32[16,16,128]{2,1,0:T(8,128)S(1)} %coarse.3), channel_id=1, replica_groups=mesh['zh'=2,'y'=4,'x'=4,'zl'=8,'core'=2] {'zl','core'}, dimensions={0} | all-to-all | bytes 262144 | tf_op jit(solution)/shard_map/all_to_all | solution.py:368
  227.0 3.8 %collective-permute-start.13 = (f32[256,128]{1,0:T(8,128)S(1)}, f32[256,128]{1,0:T(8,128)S(1)}, u32[]{:S(2)}, u32[]{:S(2)}) collective-permute-start(f32[256,128]{1,0:T(8,128)S(1)} %get-tuple-element.79), channel_id=1, source_target_pairs={{0,496},{16,32},{32,16},{48,64},{64,48},{80,96},{96,80},{112,128},... | collective-permute-start | bytes 393224 | tf_op jit(solution)/shard_map/ppermute | solution.py:333
  234.7 5.3 %collective-permute-start.16 = (f32[256,128]{1,0:T(8,128)S(1)}, f32[256,128]{1,0:T(8,128)S(1)}, u32[]{:S(2)}, u32[]{:S(2)}) collective-permute-start(f32[256,128]{1,0:T(8,128)S(1)} %get-tuple-element.82), channel_id=1, source_target_pairs={{0,1},{1,0},{2,3},{3,2},{4,5},{5,4},{6,7},{7,6},{8,9},{9,8},{10,11... | collective-permute-start | bytes 393224 | tf_op jit(solution)/shard_map/ppermute | solution.py:336
  240.0 23.3 %all_to_all.54.parts_ref = f32[32,1,128]{2,1,0:T(1,128)S(1)} all-to-all(f32[32,1,128]{2,1,0:T(1,128)S(1)} %get-tuple-element.76), channel_id=1, replica_groups=mesh['zh'=2,'y'=4,'x'=4,'zl'=8,'core'=2] {'zh','zl','core'}, dimensions={0} | all-to-all | bytes 32768 | tf_op jit(solution)/shard_map/all_to_all | solution.py:341
  263.3 12.0 %all_to_all.55.refs_0_.over_ref = f32[16,1,128]{2,1,0:T(1,128)S(1)} all-to-all(f32[16,1,128]{2,1,0:T(1,128)S(1)} %sum.4), channel_id=1, replica_groups=mesh['zh'=2,'y'=4,'x'=4,'zl'=8,'core'=2] {'y','x'}, dimensions={0} | all-to-all | bytes 16384 | tf_op jit(solution)/shard_map/all_to_all | solution.py:343
  275.3 2.3 direction_again.1
  277.7 3.6 %collective-permute-start.17 = (f32[256,128]{1,0:T(8,128)S(1)}, f32[256,128]{1,0:T(8,128)S(1)}, u32[]{:S(2)}, u32[]{:S(2)}) collective-permute-start(f32[256,128]{1,0:T(8,128)S(1)} %get-tuple-element.86), channel_id=1, source_target_pairs={{0,496},{16,0},{32,16},{48,32},{64,48},{80,64},{96,80},{112,96},{1... | collective-permute-start | bytes 393224 | tf_op jit(solution)/shard_map/ppermute | solution.py:405
  281.3 4.3 %collective-permute-start.18 = (f32[256,128]{1,0:T(8,128)S(1)}, f32[256,128]{1,0:T(8,128)S(1)}, u32[]{:S(2)}, u32[]{:S(2)}) collective-permute-start(f32[256,128]{1,0:T(8,128)S(1)} %get-tuple-element.87), channel_id=1, source_target_pairs={{0,15},{1,0},{2,1},{3,2},{4,3},{5,4},{6,5},{7,6},{8,7},{9,8},{10,9... | collective-permute-start | bytes 393224 | tf_op jit(solution)/shard_map/ppermute | solution.py:406
  285.6 23.3 %all_to_all.56.parts_ref = f32[32,1,128]{2,1,0:T(1,128)S(1)} all-to-all(f32[32,1,128]{2,1,0:T(1,128)S(1)} %get-tuple-element.83), channel_id=1, replica_groups=mesh['zh'=2,'y'=4,'x'=4,'zl'=8,'core'=2] {'zh','zl','core'}, dimensions={0} | all-to-all | bytes 32768 | tf_op jit(solution)/shard_map/all_to_all | solution.py:341
  309.0 8.9 %all_to_all.57.under_ref = f32[16,1,128]{2,1,0:T(1,128)S(1)} all-to-all(f32[16,1,128]{2,1,0:T(1,128)S(1)} %sum.5), channel_id=1, replica_groups=mesh['zh'=2,'y'=4,'x'=4,'zl'=8,'core'=2] {'y','x'}, dimensions={0} | all-to-all | bytes 16384 | tf_op jit(solution)/shard_map/all_to_all | solution.py:343
  (77 shorter events, 30.1 us)
Async XLA Ops:
  1.8 1.0 copy-start.1
  3.5 38.6 %collective-permute-start.3 = (f32[528,128]{1,0:T(8,128)S(1)}, f32[528,128]{1,0:T(8,128)S(1)}, u32[]{:S(2)}, u32[]{:S(2)}) collective-permute-start(f32[528,128]{1,0:T(8,128)S(1)} %get-tuple-element.50), channel_id=1, source_target_pairs={{0,15},{1,2},{2,1},{3,4},{4,3},{5,6},{6,5},{7,8},{8,7},{9,10},{10,... | collective-permute-start | bytes 811016 | tf_op jit(solution)/shard_map/ppermute | solution.py:334
  8.5 33.7 %collective-permute-start.4 = (f32[528,128]{1,0:T(8,128)S(1)}, f32[528,128]{1,0:T(8,128)S(1)}, u32[]{:S(2)}, u32[]{:S(2)}) collective-permute-start(f32[528,128]{1,0:T(8,128)S(1)} %get-tuple-element.51), channel_id=1, source_target_pairs={{0,1},{1,0},{2,3},{3,2},{4,5},{5,4},{6,7},{7,6},{8,9},{9,8},{10,11... | collective-permute-start | bytes 811016 | tf_op jit(solution)/shard_map/ppermute | solution.py:336
  19.6 34.1 %collective-permute-start = (f32[256,128]{1,0:T(8,128)S(1)}, f32[256,128]{1,0:T(8,128)S(1)}, u32[]{:S(2)}, u32[]{:S(2)}) collective-permute-start(f32[256,128]{1,0:T(8,128)S(1)} %get-tuple-element.46.first_ref), channel_id=1, source_target_pairs={{0,16},{16,32},{32,48},{48,64},{64,80},{80,96},{96,112},{112,128},... | collective-permute-start | bytes 393224 | tf_op jit(solution)/shard_map/ppermute | solution.py:355
  22.7 31.0 %collective-permute-start.1 = (bf16[272,128]{1,0:T(8,128)(2,1)S(1)}, bf16[272,128]{1,0:T(8,128)(2,1)S(1)}, u32[]{:S(2)}, u32[]{:S(2)}) collective-permute-start(bf16[272,128]{1,0:T(8,128)(2,1)S(1)} %get-tuple-element.48), channel_id=1, source_target_pairs={{0,496},{16,32},{32,16},{48,64},{64,48},{80,96},{96,80},{112,128},... | collective-permute-start | bytes 208904 | tf_op jit(solution)/shard_map/ppermute | solution.py:333
  37.8 15.9 %collective-permute-start.2 = (bf16[272,128]{1,0:T(8,128)(2,1)S(1)}, bf16[272,128]{1,0:T(8,128)(2,1)S(1)}, u32[]{:S(2)}, u32[]{:S(2)}) collective-permute-start(bf16[272,128]{1,0:T(8,128)(2,1)S(1)} %get-tuple-element.49), channel_id=1, source_target_pairs={{0,16},{16,0},{32,48},{48,32},{64,80},{80,64},{96,112},{112,96},{1... | collective-permute-start | bytes 208904 | tf_op jit(solution)/shard_map/ppermute | solution.py:335
  39.7 1.0 copy-start.2
  42.2 1.0 copy-start.3
  53.7 28.9 %copy-start.12 = (bf16[256,512]{1,0:T(8,128)(2,1)S(1)}, bf16[256,512]{1,0:T(8,128)(2,1)}, u32[]{:S(2)}) copy-start(bf16[256,512]{1,0:T(8,128)(2,1)} %coarse_ref.3) | copy-start | bytes 786436
  53.7 47.1 %copy-start = (bf16[1,1,1024,1024]{3,2,1,0:T(8,128)(2,1)S(1)}, bf16[1,1,1024,1024]{3,2,1,0:T(8,128)(2,1)}, u32[]{:S(2)}) copy-start(bf16[1,1,1024,1024]{3,2,1,0:T(8,128)(2,1)} %param.7) | copy-start | bytes 6291460
  58.9 43.3 %copy-start.10 = (f32[1024,128]{1,0:T(8,128)}, f32[1024,128]{1,0:T(8,128)S(1)}, u32[]{:S(2)}) copy-start(f32[1024,128]{1,0:T(8,128)S(1)} %get-tuple-element.56.residual_ref.last_ref) | copy-start | bytes 1572868
  58.9 68.0 %copy-start.5 = (f32[2,256,256]{2,1,0:T(8,128)}, f32[2,256,256]{2,1,0:T(8,128)S(1)}, u32[]{:S(2)}) copy-start(f32[2,256,256]{2,1,0:T(8,128)S(1)} %get-tuple-element.64.refs_8_.slab_factors.refs_10_) | copy-start | bytes 1572868
  82.6 44.3 %copy-start.4 = (bf16[1,1,4,256,256]{4,3,2,1,0:T(8,128)(2,1)S(1)}, bf16[1,1,4,256,256]{4,3,2,1,0:T(8,128)(2,1)}, u32[]{:S(2)}) copy-start(bf16[1,1,4,256,256]{4,3,2,1,0:T(8,128)(2,1)} %param.6) | copy-start | bytes 1572868
  102.2 24.7 %collective-permute-start.5 = (f32[256,128]{1,0:T(8,128)S(1)}, f32[256,128]{1,0:T(8,128)S(1)}, u32[]{:S(2)}, u32[]{:S(2)}) collective-permute-start(f32[256,128]{1,0:T(8,128)S(1)} %get-tuple-element.60), channel_id=1, source_target_pairs={{0,496},{16,32},{32,16},{48,64},{64,48},{80,96},{96,80},{112,128},... | collective-permute-start | bytes 393224 | tf_op jit(solution)/shard_map/ppermute | solution.py:333
  108.0 18.9 %collective-permute-start.6 = (f32[256,128]{1,0:T(8,128)S(1)}, f32[256,128]{1,0:T(8,128)S(1)}, u32[]{:S(2)}, u32[]{:S(2)}) collective-permute-start(f32[256,128]{1,0:T(8,128)S(1)} %get-tuple-element.61), channel_id=1, source_target_pairs={{0,15},{1,2},{2,1},{3,4},{4,3},{5,6},{6,5},{7,8},{8,7},{9,10},{10,... | collective-permute-start | bytes 393224 | tf_op jit(solution)/shard_map/ppermute | solution.py:334
  109.9 17.0 %collective-permute-start.7 = (f32[256,128]{1,0:T(8,128)S(1)}, f32[256,128]{1,0:T(8,128)S(1)}, u32[]{:S(2)}, u32[]{:S(2)}) collective-permute-start(f32[256,128]{1,0:T(8,128)S(1)} %get-tuple-element.62), channel_id=1, source_target_pairs={{0,16},{16,0},{32,48},{48,32},{64,80},{80,64},{96,112},{112,96},{1... | collective-permute-start | bytes 393224 | tf_op jit(solution)/shard_map/ppermute | solution.py:335
  111.8 15.0 %collective-permute-start.8 = (f32[256,128]{1,0:T(8,128)S(1)}, f32[256,128]{1,0:T(8,128)S(1)}, u32[]{:S(2)}, u32[]{:S(2)}) collective-permute-start(f32[256,128]{1,0:T(8,128)S(1)} %get-tuple-element.63), channel_id=1, source_target_pairs={{0,1},{1,0},{2,3},{3,2},{4,5},{5,4},{6,7},{7,6},{8,9},{9,8},{10,11... | collective-permute-start | bytes 393224 | tf_op jit(solution)/shard_map/ppermute | solution.py:336
  134.0 29.3 %all-to-all-start.2 = ((f32[32,2,128]{2,1,0:T(2,128)}), f32[32,2,128]{2,1,0:T(2,128)S(1)}, u32[]{:S(2)}, u32[]{:S(2)}) async-start(f32[32,2,128]{2,1,0:T(2,128)} %get-tuple-element.66), calls=%async_computation.2 | async-start | bytes 65536 | tf_op jit(solution)/shard_map/all_to_all | solution.py:341
  142.1 26.5 %collective-permute-start.9 = (f32[256,128]{1,0:T(8,128)}, f32[256,128]{1,0:T(8,128)}, u32[]{:S(2)}, u32[]{:S(2)}) collective-permute-start(f32[256,128]{1,0:T(8,128)} %copy-done.20), channel_id=1, source_target_pairs={{0,496},{16,32},{32,16},{48,64},{64,48},{80,96},{96,80},{112,128},... | collective-permute-start | bytes 393224 | tf_op jit(solution)/shard_map/ppermute | solution.py:333
  156.7 15.6 %collective-permute-start.10 = (f32[256,128]{1,0:T(8,128)}, f32[256,128]{1,0:T(8,128)}, u32[]{:S(2)}, u32[]{:S(2)}) collective-permute-start(f32[256,128]{1,0:T(8,128)} %copy-done.19), channel_id=1, source_target_pairs={{0,15},{1,2},{2,1},{3,4},{4,3},{5,6},{6,5},{7,8},{8,7},{9,10},{10,... | collective-permute-start | bytes 393224 | tf_op jit(solution)/shard_map/ppermute | solution.py:334
  159.4 12.8 %collective-permute-start.11 = (f32[256,128]{1,0:T(8,128)}, f32[256,128]{1,0:T(8,128)}, u32[]{:S(2)}, u32[]{:S(2)}) collective-permute-start(f32[256,128]{1,0:T(8,128)} %copy-done.18), channel_id=1, source_target_pairs={{0,16},{16,0},{32,48},{48,32},{64,80},{80,64},{96,112},{112,96},{1... | collective-permute-start | bytes 393224 | tf_op jit(solution)/shard_map/ppermute | solution.py:335
  161.3 10.9 %collective-permute-start.12 = (f32[256,128]{1,0:T(8,128)}, f32[256,128]{1,0:T(8,128)}, u32[]{:S(2)}, u32[]{:S(2)}) collective-permute-start(f32[256,128]{1,0:T(8,128)} %copy-done.17), channel_id=1, source_target_pairs={{0,1},{1,0},{2,3},{3,2},{4,5},{5,4},{6,7},{7,6},{8,9},{9,8},{10,11... | collective-permute-start | bytes 393224 | tf_op jit(solution)/shard_map/ppermute | solution.py:336
  163.9 11.0 %all-to-all-start.3 = ((f32[16,2,128]{2,1,0:T(2,128)}), f32[16,2,128]{2,1,0:T(2,128)S(1)}, u32[]{:S(2)}, u32[]{:S(2)}) async-start(f32[16,2,128]{2,1,0:T(2,128)} %sum.3), calls=%async_computation.3 | async-start | bytes 32768 | tf_op jit(solution)/shard_map/all_to_all | solution.py:343
  174.9 1.0 copy-start.6
  207.4 67.9 %copy-start.7 = (f32[2,256,256]{2,1,0:T(8,128)S(1)}, f32[2,256,256]{2,1,0:T(8,128)}, u32[]{:S(2)}) copy-start(f32[2,256,256]{2,1,0:T(8,128)} %copy-done.5) | copy-start | bytes 1572868
  207.4 68.0 %copy-start.9 = (f32[1024,128]{1,0:T(8,128)S(1)}, f32[1024,128]{1,0:T(8,128)}, u32[]{:S(2)}) copy-start(f32[1024,128]{1,0:T(8,128)} %copy-done.8) | copy-start | bytes 1572868
  227.0 48.2 %collective-permute-start.13 = (f32[256,128]{1,0:T(8,128)S(1)}, f32[256,128]{1,0:T(8,128)S(1)}, u32[]{:S(2)}, u32[]{:S(2)}) collective-permute-start(f32[256,128]{1,0:T(8,128)S(1)} %get-tuple-element.79), channel_id=1, source_target_pairs={{0,496},{16,32},{32,16},{48,64},{64,48},{80,96},{96,80},{112,128},... | collective-permute-start | bytes 393224 | tf_op jit(solution)/shard_map/ppermute | solution.py:333
  230.8 44.5 %collective-permute-start.14 = (f32[256,128]{1,0:T(8,128)S(1)}, f32[256,128]{1,0:T(8,128)S(1)}, u32[]{:S(2)}, u32[]{:S(2)}) collective-permute-start(f32[256,128]{1,0:T(8,128)S(1)} %get-tuple-element.80), channel_id=1, source_target_pairs={{0,15},{1,2},{2,1},{3,4},{4,3},{5,6},{6,5},{7,8},{8,7},{9,10},{10,... | collective-permute-start | bytes 393224 | tf_op jit(solution)/shard_map/ppermute | solution.py:334
  232.8 42.5 %collective-permute-start.15 = (f32[256,128]{1,0:T(8,128)S(1)}, f32[256,128]{1,0:T(8,128)S(1)}, u32[]{:S(2)}, u32[]{:S(2)}) collective-permute-start(f32[256,128]{1,0:T(8,128)S(1)} %get-tuple-element.81), channel_id=1, source_target_pairs={{0,16},{16,0},{32,48},{48,32},{64,80},{80,64},{96,112},{112,96},{1... | collective-permute-start | bytes 393224 | tf_op jit(solution)/shard_map/ppermute | solution.py:335
  234.7 40.6 %collective-permute-start.16 = (f32[256,128]{1,0:T(8,128)S(1)}, f32[256,128]{1,0:T(8,128)S(1)}, u32[]{:S(2)}, u32[]{:S(2)}) collective-permute-start(f32[256,128]{1,0:T(8,128)S(1)} %get-tuple-element.82), channel_id=1, source_target_pairs={{0,1},{1,0},{2,3},{3,2},{4,5},{5,4},{6,7},{7,6},{8,9},{9,8},{10,11... | collective-permute-start | bytes 393224 | tf_op jit(solution)/shard_map/ppermute | solution.py:336
  277.7 40.3 %collective-permute-start.17 = (f32[256,128]{1,0:T(8,128)S(1)}, f32[256,128]{1,0:T(8,128)S(1)}, u32[]{:S(2)}, u32[]{:S(2)}) collective-permute-start(f32[256,128]{1,0:T(8,128)S(1)} %get-tuple-element.86), channel_id=1, source_target_pairs={{0,496},{16,0},{32,16},{48,32},{64,48},{80,64},{96,80},{112,96},{1... | collective-permute-start | bytes 393224 | tf_op jit(solution)/shard_map/ppermute | solution.py:405
  281.3 36.6 %collective-permute-start.18 = (f32[256,128]{1,0:T(8,128)S(1)}, f32[256,128]{1,0:T(8,128)S(1)}, u32[]{:S(2)}, u32[]{:S(2)}) collective-permute-start(f32[256,128]{1,0:T(8,128)S(1)} %get-tuple-element.87), channel_id=1, source_target_pairs={{0,15},{1,0},{2,1},{3,2},{4,3},{5,4},{6,5},{7,6},{8,7},{9,8},{10,9... | collective-permute-start | bytes 393224 | tf_op jit(solution)/shard_map/ppermute | solution.py:406
  (10 other events, 7.9 us)

commit v3 on v2

--- a/solution.py
+++ b/solution.py
@@ -121,7 +121,8 @@
     out_ref[:HALF, HALF:] = out_ref[:HALF, HALF:] + below.T
 
 
-def primal_kernel(ids_ref, blocks_ref, primal_ref):
+def primal_kernel(even_ref, ids_ref, blocks_ref, coarse_ref, after_ref, primal_ref, sent_ref):
+    sent_ref[...] = jnp.where(even_ref[2] == 1, coarse_ref[:, :F], coarse_ref[:, F:])
     row = lax.broadcasted_iota(jnp.int32, (PRIM, NI), 0)
     picked = jnp.zeros((PRIM, NI), jnp.int32)
     for k in range(PRIM):
@@ -158,14 +159,21 @@
         lifted_ref[rows(k)] = fine_dot(factors_ref[k], residual_ref[rows(k)])
 
 
-def begin_kernel(even_ref, from_slab, slab_b, slab_a, blocks_ref, first_ref, primal_ref, patch_residual_ref,
-                 patch_lifted_ref, factors_ref, residual_ref, lifted_ref, rounded_ref, c_ref, a_ref, some_ref, solved_ref):
+def begin_kernel(even_ref, from_slab, slab_b, slab_a, blocks_ref, first_ref, patch_residual_ref,
+                 patch_lifted_ref, factors_ref, residual_ref, lifted_ref, rounded_ref, a_ref, some_ref, solved_ref):
     invert_kernel(0, even_ref, slab_b, slab_a, blocks_ref, first_ref, from_slab, factors_ref, some_ref, solved_ref, a_ref)
     for k in range(2):
         for flag, part, solved in ((0, some_ref, solved_ref), (1, patch_residual_ref, patch_lifted_ref)):
             residual_ref[rows(2 * k + flag)] = part[rows(k)]
             lifted_ref[rows(2 * k + flag)] = solved[rows(k)]
     rounded_ref[...] = lifted_ref[...].astype(jnp.bfloat16)
+
+
+def merge_kernel(even_ref, kept_ref, swapped_ref, primal_ref, rounded_ref, c_ref, coarse_ref):
+    high = even_ref[2] == 1
+    kept = jnp.where(high, kept_ref[:, F:], kept_ref[:, :F])
+    coarse_ref[:F] = jnp.where(high, swapped_ref[...], kept)
+    coarse_ref[F:] = jnp.where(high, kept, swapped_ref[...])
     restrict(primal_ref, rounded_ref, c_ref)
 
 
@@ -246,8 +254,10 @@
 
 
 def coarse_kernel(coarse_ref, gathered_ref, out_ref):
-    gathered = gathered_ref[...].reshape(OWN, RHS)
-    out_ref[...] = rough_dot(coarse_ref[...], gathered).reshape(16, PRIM, RHS)
+    gathered = gathered_ref[...].reshape(2 * F, RHS)
+    out_ref[...] = lax.dot_general(
+        coarse_ref[...], gathered, (((0,), (0,)), ((), ())), preferred_element_type=jnp.float32
+    ).reshape(16, PRIM, RHS)
 
 
 def repeat_rows(out_ref, value):
@@ -349,23 +359,25 @@
     ids = primal_ids[0, 0]
     slab_even = 1 - lax.axis_index("x") % 2
     patch_even = 1 - lax.axis_index("core")
-    even = jnp.stack([slab_even, patch_even]).astype(jnp.int32)
+    even = jnp.stack([slab_even, patch_even, lax.axis_index("zh")]).astype(jnp.int32)
 
     first, second = call(turn_kernel, [f32(F, RHS)] * 2, [VMEM], "turn")(rhs[0, 0])
     from_slab = lax.ppermute(first, SLAB, roll_pairs(32, 1))
     send = call(
         pack_kernel, [bf16(PACKED, HALF), f32(PACKED + F, HALF)] * 2, [SMEM, VMEM, VMEM], "pack")(even, second, blocks)
     got = swap(send)
-    primal = call(primal_kernel, bf16(PRIM, NI), [SMEM, VMEM], "primal")(ids, blocks)
+    primal, *sent = call(primal_kernel, [bf16(PRIM, NI), bf16(F, F)], [SMEM, SMEM, VMEM, VMEM, pl.BlockSpec(memory_space=pl.ANY)], "primal")(
+        even, ids, blocks, coarse_inverse, got[3])
+    swapped = lax.ppermute(sent[0], "zh", [(0, 1), (1, 0)])
     field = f32(NI, RHS)
     part = [f32(F, RHS)] * 4
     solved = [field, field, bf16(NI, RHS), bf16(32, PRIM, RHS)]
     solve_flops = 4 * 12 * F * F * RHS
 
     def coarse_terms(residual, lifted, rounded, c):
-        gathered = lax.all_to_all(c, SLAB, 0, 0)
-        partial = call(coarse_kernel, f32(16, PRIM, RHS), [VMEM] * 2, "coarse", 1 << 25)(coarse_inverse, gathered)
-        parts = lax.all_to_all(partial, PATCH, 0, 0)
+        gathered = lax.all_to_all(c, COLUMN, 0, 0)
+        partial = call(coarse_kernel, f32(16, PRIM, RHS), [VMEM] * 2, "coarse", 1 << 25)(coarse, gathered)
+        parts = lax.all_to_all(partial, PLANE, 0, 0)
         terms, product, *send = call(
             terms_kernel, [field, f32(32, 1, RHS)] + part, [SMEM] + [VMEM] * 6, "terms", 1 << 28)(
                 even, parts, inverse, rounded, primal, residual, lifted)
@@ -378,10 +390,12 @@
         lambda even_ref, part_b, part_a, blocks_ref, right_ref, *refs: invert_kernel(
             1, even_ref, part_b, part_a, blocks_ref, right_ref, None, *refs),
         pair, [SMEM] + [VMEM] * 4, "invert", 1 << 32, [square])(even, got[1], got[3], blocks, second)
-    slab_factors, residual, lifted, rounded, c = call(
-        begin_kernel, pair[:1] + solved, [SMEM] + [VMEM] * 8, "begin", 1 << 32,
+    slab_factors, residual, lifted, rounded = call(
+        begin_kernel, pair[:1] + solved[:3], [SMEM] + [VMEM] * 7, "begin", 0,
         [square, pltpu.VMEM((2 * F, RHS), jnp.float32), pltpu.VMEM((2 * F, RHS), jnp.float32)])(
-            even, from_slab, got[0], got[2], blocks, first, primal, patch_residual, patch_lifted)
+            even, from_slab, got[0], got[2], blocks, first, patch_residual, patch_lifted)
+    c, coarse = call(merge_kernel, [solved[3], bf16(2 * F, F)], [SMEM] + [VMEM] * 4, "merge")(
+        even, coarse_inverse, swapped, primal, rounded)
     factors = (slab_factors, patch_factors)
     terms, product, send = coarse_terms(residual, lifted, rounded, c)
     got = swap(send)

time: 320 us -> 311 us (0.972)
  blocking collectives: 154 us -> 139 us
  starting transfers between devices: 106 us -> 121 us
  waiting for transfers between devices: 21.7 us -> 9.69 us
    ppermute x4, waiting for transfers between devices: 15.4 us -> 3.23 us  [swap(): lax.ppermute(slab_b, SLAB, even_pairs(32))]
    all_to_all x4, blocking collectives: 86.7 us -> 74.8 us  [the longest x2 55.6 us: coarse_terms(): gathered = lax.all_to_all(c, COLUMN, 0, 0)]
    ppermute x0 -> x1, starting transfers between devices: none -> 10.7 us  [on_device(): swapped = lax.ppermute(sent[0], 'zh', [(0, 1), (1, 0)])]
    all_to_all x1, starting transfers between devices: 8.04 us -> 13.8 us  [total_parts(): parts = lax.all_to_all(spread, COLUMN, 0, 0)]
    all_to_all x2, blocking collectives: 46.6 us -> 43.2 us  [total_parts(): parts = lax.all_to_all(spread, COLUMN, 0, 0)]
    ppermute x4, starting transfers between devices: 11.5 us -> 14.8 us  [swap(): lax.ppermute(patch_b, PATCH, even_pairs(16))]
    unnamed x42 -> x44, local copies, waits for them, and re-layouts: 12 us -> 13 us
    pallas_call x2 -> x3, Pallas kernels: 5.94 us -> 6.48 us  [the longest x1 5.03 us: on_device(): call(begin_kernel, pair[:1] + solved[:3], [SMEM] + [VMEM] * 7, 'begin', 0...]
  transfers between devices with their start and end apart: 21 -> 22, of which waited for: 4 -> 3; matrix products, arithmetic and copies ran while one was open for 0% -> 0% of each run, Pallas kernels for 2% -> 4%
where the time goes in v3:
time: 311 us; the launch traced here: 309 us
  blocking collectives  139 us (45%)
  starting transfers between devices  121 us (39%)
  Pallas kernels  24.9 us (8%)
  local copies, waits for them, and re-layouts  13 us (4%)
  waiting for transfers between devices  9.69 us (3%)
    all_to_all x2, blocking collectives, coarse_terms(): gathered = lax.all_to_all(c, COLUMN, 0, 0)  55.6 us
    all_to_all x2, blocking collectives, total_parts(): parts = lax.all_to_all(spread, COLUMN, 0, 0)  43.2 us
    ppermute x4, starting transfers between devices, swap(): lax.ppermute(slab_b, SLAB, even_pairs(32))  38.2 us
    all_to_all x2, blocking collectives, total_parts(): return lax.all_to_all(spread, PLANE, 0, 0)  21.2 us
    ppermute x4, starting transfers between devices, swap(): lax.ppermute(patch_a, PATCH, odd_pairs(16))  20.8 us
    all_to_all x2, blocking collectives, coarse_terms(): parts = lax.all_to_all(partial, PLANE, 0, 0)  19.1 us
    ppermute x4, starting transfers between devices, swap(): lax.ppermute(patch_b, PATCH, even_pairs(16))  14.8 us
    all_to_all x1, starting transfers between devices, total_parts(): parts = lax.all_to_all(spread, COLUMN, 0, 0)  13.8 us
  transfers between devices with their start and end apart: 22, of which 3 were waited for; matrix products, arithmetic and copies ran while one was open for 0% of the time, Pallas kernels for 4%

profile of v3, /device:TPU:1, one launch (start us, length us, event | category | flops | bytes accessed | tf_op | source)
XLA Modules:
  0.0 309.4 jit_solution(17103637876573943449)
XLA Ops:
  3.6 8.8 %collective-permute-start = (f32[528,128]{1,0:T(8,128)S(1)}, f32[528,128]{1,0:T(8,128)S(1)}, u32[]{:S(2)}, u32[]{:S(2)}) collective-permute-start(f32[528,128]{1,0:T(8,128)S(1)} %get-tuple-element.50), channel_id=1, source_target_pairs={{0,1},{1,0},{2,3},{3,2},{4,5},{5,4},{6,7},{7,6},{8,9},{9,8},{10,11... | collective-permute-start | bytes 811016 | tf_op jit(solution)/shard_map/ppermute | solution.py:346
  16.2 16.3 %collective-permute-start.3 = (bf16[272,128]{1,0:T(8,128)(2,1)S(1)}, bf16[272,128]{1,0:T(8,128)(2,1)S(1)}, u32[]{:S(2)}, u32[]{:S(2)}) collective-permute-start(bf16[272,128]{1,0:T(8,128)(2,1)S(1)} %get-tuple-element.54), channel_id=1, source_target_pairs={{0,496},{16,32},{32,16},{48,64},{64,48},{80,96},{96,80},{112,128},... | collective-permute-start | bytes 208904 | tf_op jit(solution)/shard_map/ppermute | solution.py:343
  37.8 10.7 %collective-permute-start.1 = (bf16[256,256]{1,0:T(8,128)(2,1)S(1)}, bf16[256,256]{1,0:T(8,128)(2,1)S(1)}, u32[]{:S(2)}, u32[]{:S(2)}) collective-permute-start(bf16[256,256]{1,0:T(8,128)(2,1)S(1)} %get-tuple-element.51), channel_id=1, source_target_pairs={{0,256},{256,0},{1,257},{257,1},{2,258},{258,2},{3,259},{259,3},{4... | collective-permute-start | bytes 393224 | tf_op jit(solution)/shard_map/ppermute | solution.py:371
  49.6 4.9 %invert.1 = (f32[2,256,256]{2,1,0:T(8,128)S(1)}, f32[512,128]{1,0:T(8,128)S(1)}, f32[512,128]{1,0:T(8,128)S(1)}) custom-call(s32[3]{0:T(128)S(1)} %pad_add_fusion.even_ref.refs_1_.refs_3_, f32[528,128]{1,0:T(8,128)S(1)} %collective-permute-done.5.part_b, f32[528,128]{1,0:T(8,128)S(1)} %collective-permute-done.after_ref.part_a, ...), custom_call_target="tpu_custom_call" | custom-call | flops 4294967296 | bytes 1048576 | tf_op jit(solution)/shard_map/invert/pallas_call | solution.py:389
  54.5 5.0 %begin.1 = (f32[2,256,256]{2,1,0:T(8,128)S(1)}, f32[1024,128]{1,0:T(8,128)S(1)}, f32[1024,128]{1,0:T(8,128)S(1)}, bf16[1024,128]{1,0:T(8,128)(2,1)S(1)}) custom-call(s32[3]{0:T(128)S(1)} %pad_add_fusion.even_ref.refs_1_.refs_3_, f32[256,128]{1,0:T(8,128)S(1)} %collective-permute-done.2.from_slab, bf16[272,128]{1,0:T(8,128)(2,1)S(1)} %collective-permute-done.3.slab_b, ...), custom_call_target="tpu_custom_call" | custom-call | bytes 1048576 | tf_op jit(solution)/shard_map/begin/pallas_call | solution.py:393
  60.3 28.8 %all_to_all.50.gathered_ref = bf16[32,16,128]{2,1,0:T(8,128)(2,1)S(1)} all-to-all(bf16[32,16,128]{2,1,0:T(8,128)(2,1)S(1)} %get-tuple-element.61), channel_id=1, replica_groups=mesh['zh'=2,'y'=4,'x'=4,'zl'=8,'core'=2] {'zh','zl','core'}, dimensions={0} | all-to-all | bytes 262144 | tf_op jit(solution)/shard_map/all_to_all | solution.py:378
  89.4 9.4 %all_to_all.51.parts_ref = f32[16,16,128]{2,1,0:T(8,128)S(1)} all-to-all(f32[16,16,128]{2,1,0:T(8,128)S(1)} %coarse.2), channel_id=1, replica_groups=mesh['zh'=2,'y'=4,'x'=4,'zl'=8,'core'=2] {'y','x'}, dimensions={0} | all-to-all | bytes 262144 | tf_op jit(solution)/shard_map/all_to_all | solution.py:380
  100.2 4.1 %collective-permute-start.6 = (f32[256,128]{1,0:T(8,128)S(1)}, f32[256,128]{1,0:T(8,128)S(1)}, u32[]{:S(2)}, u32[]{:S(2)}) collective-permute-start(f32[256,128]{1,0:T(8,128)S(1)} %get-tuple-element.66), channel_id=1, source_target_pairs={{0,496},{16,32},{32,16},{48,64},{64,48},{80,96},{96,80},{112,128},... | collective-permute-start | bytes 393224 | tf_op jit(solution)/shard_map/ppermute | solution.py:343
  104.3 5.0 %collective-permute-start.7 = (f32[256,128]{1,0:T(8,128)S(1)}, f32[256,128]{1,0:T(8,128)S(1)}, u32[]{:S(2)}, u32[]{:S(2)}) collective-permute-start(f32[256,128]{1,0:T(8,128)S(1)} %get-tuple-element.67), channel_id=1, source_target_pairs={{0,15},{1,2},{2,1},{3,4},{4,3},{5,6},{6,5},{7,8},{8,7},{9,10},{10,... | collective-permute-start | bytes 393224 | tf_op jit(solution)/shard_map/ppermute | solution.py:344
  111.3 5.0 %collective-permute-start.9 = (f32[256,128]{1,0:T(8,128)S(1)}, f32[256,128]{1,0:T(8,128)S(1)}, u32[]{:S(2)}, u32[]{:S(2)}) collective-permute-start(f32[256,128]{1,0:T(8,128)S(1)} %get-tuple-element.69), channel_id=1, source_target_pairs={{0,1},{1,0},{2,3},{3,2},{4,5},{5,4},{6,7},{7,6},{8,9},{9,8},{10,11... | collective-permute-start | bytes 393224 | tf_op jit(solution)/shard_map/ppermute | solution.py:346
  116.3 3.2 %collective-permute-done.6.refs_3_ = f32[256,128]{1,0:T(8,128)S(1)} collective-permute-done((f32[256,128]{1,0:T(8,128)S(1)}, f32[256,128]{1,0:T(8,128)S(1)}, u32[]{:S(2)}, u32[]{:S(2)}) %collective-permute-start.6) | collective-permute-done | bytes 131104 | tf_op jit(solution)/shard_map/ppermute | solution.py:343
  119.6 2.9 direction.1
  126.7 13.8 %all-to-all-start.2 = ((f32[32,2,128]{2,1,0:T(2,128)}), f32[32,2,128]{2,1,0:T(2,128)S(1)}, u32[]{:S(2)}, u32[]{:S(2)}) async-start(f32[32,2,128]{2,1,0:T(2,128)} %get-tuple-element.72), calls=%async_computation.2 | async-start | bytes 65536 | tf_op jit(solution)/shard_map/all_to_all | solution.py:351
  140.5 13.7 %collective-permute-start.10 = (f32[256,128]{1,0:T(8,128)}, f32[256,128]{1,0:T(8,128)}, u32[]{:S(2)}, u32[]{:S(2)}) collective-permute-start(f32[256,128]{1,0:T(8,128)} %copy-done.21), channel_id=1, source_target_pairs={{0,496},{16,32},{32,16},{48,64},{64,48},{80,96},{96,80},{112,128},... | collective-permute-start | bytes 393224 | tf_op jit(solution)/shard_map/ppermute | solution.py:343
  154.3 2.7 collective-permute-start.11
  157.0 1.9 collective-permute-start.12
  161.5 5.6 %all-to-all-start.3 = ((f32[16,2,128]{2,1,0:T(2,128)}), f32[16,2,128]{2,1,0:T(2,128)S(1)}, u32[]{:S(2)}, u32[]{:S(2)}) async-start(f32[16,2,128]{2,1,0:T(2,128)} %sum.3), calls=%async_computation.3 | async-start | bytes 32768 | tf_op jit(solution)/shard_map/all_to_all | solution.py:353
  167.1 2.7 collective-permute-done.11.patch_b
  169.8 3.7 %all-to-all-done.3.sums_ref.refs_1_.first_ref = f32[16,2,128]{2,1,0:T(2,128)S(1)} async-done(((f32[16,2,128]{2,1,0:T(2,128)}), f32[16,2,128]{2,1,0:T(2,128)S(1)}, u32[]{:S(2)}, u32[]{:S(2)}) %all-to-all-start.3) | async-done | bytes 16416 | tf_op jit(solution)/shard_map/all_to_all | solution.py:353
  176.6 2.4 update.1
  179.0 26.9 %all_to_all.52.gathered_ref = bf16[32,16,128]{2,1,0:T(8,128)(2,1)S(1)} all-to-all(bf16[32,16,128]{2,1,0:T(8,128)(2,1)S(1)} %get-tuple-element.78), channel_id=1, replica_groups=mesh['zh'=2,'y'=4,'x'=4,'zl'=8,'core'=2] {'zh','zl','core'}, dimensions={0} | all-to-all | bytes 262144 | tf_op jit(solution)/shard_map/all_to_all | solution.py:378
  206.2 9.7 %all_to_all.53.parts_ref = f32[16,16,128]{2,1,0:T(8,128)S(1)} all-to-all(f32[16,16,128]{2,1,0:T(8,128)S(1)} %coarse.3), channel_id=1, replica_groups=mesh['zh'=2,'y'=4,'x'=4,'zl'=8,'core'=2] {'y','x'}, dimensions={0} | all-to-all | bytes 262144 | tf_op jit(solution)/shard_map/all_to_all | solution.py:380
  217.2 4.1 %collective-permute-start.14 = (f32[256,128]{1,0:T(8,128)S(1)}, f32[256,128]{1,0:T(8,128)S(1)}, u32[]{:S(2)}, u32[]{:S(2)}) collective-permute-start(f32[256,128]{1,0:T(8,128)S(1)} %get-tuple-element.85), channel_id=1, source_target_pairs={{0,496},{16,32},{32,16},{48,64},{64,48},{80,96},{96,80},{112,128},... | collective-permute-start | bytes 393224 | tf_op jit(solution)/shard_map/ppermute | solution.py:343
  221.4 5.2 %collective-permute-start.15 = (f32[256,128]{1,0:T(8,128)S(1)}, f32[256,128]{1,0:T(8,128)S(1)}, u32[]{:S(2)}, u32[]{:S(2)}) collective-permute-start(f32[256,128]{1,0:T(8,128)S(1)} %get-tuple-element.86), channel_id=1, source_target_pairs={{0,15},{1,2},{2,1},{3,4},{4,3},{5,6},{6,5},{7,8},{8,7},{9,10},{10,... | collective-permute-start | bytes 393224 | tf_op jit(solution)/shard_map/ppermute | solution.py:344
  228.5 5.0 %collective-permute-start.17 = (f32[256,128]{1,0:T(8,128)S(1)}, f32[256,128]{1,0:T(8,128)S(1)}, u32[]{:S(2)}, u32[]{:S(2)}) collective-permute-start(f32[256,128]{1,0:T(8,128)S(1)} %get-tuple-element.88), channel_id=1, source_target_pairs={{0,1},{1,0},{2,3},{3,2},{4,5},{5,4},{6,7},{7,6},{8,9},{9,8},{10,11... | collective-permute-start | bytes 393224 | tf_op jit(solution)/shard_map/ppermute | solution.py:346
  233.5 19.9 %all_to_all.54.parts_ref = f32[32,1,128]{2,1,0:T(1,128)S(1)} all-to-all(f32[32,1,128]{2,1,0:T(1,128)S(1)} %get-tuple-element.82), channel_id=1, replica_groups=mesh['zh'=2,'y'=4,'x'=4,'zl'=8,'core'=2] {'zh','zl','core'}, dimensions={0} | all-to-all | bytes 32768 | tf_op jit(solution)/shard_map/all_to_all | solution.py:351
  253.4 12.3 %all_to_all.55.refs_0_.over_ref = f32[16,1,128]{2,1,0:T(1,128)S(1)} all-to-all(f32[16,1,128]{2,1,0:T(1,128)S(1)} %sum.4), channel_id=1, replica_groups=mesh['zh'=2,'y'=4,'x'=4,'zl'=8,'core'=2] {'y','x'}, dimensions={0} | all-to-all | bytes 16384 | tf_op jit(solution)/shard_map/all_to_all | solution.py:353
  265.7 2.3 direction_again.1
  268.1 3.6 %collective-permute-start.18 = (f32[256,128]{1,0:T(8,128)S(1)}, f32[256,128]{1,0:T(8,128)S(1)}, u32[]{:S(2)}, u32[]{:S(2)}) collective-permute-start(f32[256,128]{1,0:T(8,128)S(1)} %get-tuple-element.92), channel_id=1, source_target_pairs={{0,496},{16,0},{32,16},{48,32},{64,48},{80,64},{96,80},{112,96},{1... | collective-permute-start | bytes 393224 | tf_op jit(solution)/shard_map/ppermute | solution.py:419
  271.7 4.3 %collective-permute-start.19 = (f32[256,128]{1,0:T(8,128)S(1)}, f32[256,128]{1,0:T(8,128)S(1)}, u32[]{:S(2)}, u32[]{:S(2)}) collective-permute-start(f32[256,128]{1,0:T(8,128)S(1)} %get-tuple-element.93), channel_id=1, source_target_pairs={{0,15},{1,0},{2,1},{3,2},{4,3},{5,4},{6,5},{7,6},{8,7},{9,8},{10,9... | collective-permute-start | bytes 393224 | tf_op jit(solution)/shard_map/ppermute | solution.py:420
  276.0 23.3 %all_to_all.56.parts_ref = f32[32,1,128]{2,1,0:T(1,128)S(1)} all-to-all(f32[32,1,128]{2,1,0:T(1,128)S(1)} %get-tuple-element.89), channel_id=1, replica_groups=mesh['zh'=2,'y'=4,'x'=4,'zl'=8,'core'=2] {'zh','zl','core'}, dimensions={0} | all-to-all | bytes 32768 | tf_op jit(solution)/shard_map/all_to_all | solution.py:351
  299.4 8.9 %all_to_all.57.under_ref = f32[16,1,128]{2,1,0:T(1,128)S(1)} all-to-all(f32[16,1,128]{2,1,0:T(1,128)S(1)} %sum.5), channel_id=1, replica_groups=mesh['zh'=2,'y'=4,'x'=4,'zl'=8,'core'=2] {'y','x'}, dimensions={0} | all-to-all | bytes 16384 | tf_op jit(solution)/shard_map/all_to_all | solution.py:353
  (82 shorter events, 31.9 us)
Async XLA Ops:
  1.8 1.0 copy-start.1
  3.6 30.9 %collective-permute-start = (f32[528,128]{1,0:T(8,128)S(1)}, f32[528,128]{1,0:T(8,128)S(1)}, u32[]{:S(2)}, u32[]{:S(2)}) collective-permute-start(f32[528,128]{1,0:T(8,128)S(1)} %get-tuple-element.50), channel_id=1, source_target_pairs={{0,1},{1,0},{2,3},{3,2},{4,5},{5,4},{6,7},{7,6},{8,9},{9,8},{10,11... | collective-permute-start | bytes 811016 | tf_op jit(solution)/shard_map/ppermute | solution.py:346
  12.3 36.2 %collective-permute-start.5 = (f32[528,128]{1,0:T(8,128)S(1)}, f32[528,128]{1,0:T(8,128)S(1)}, u32[]{:S(2)}, u32[]{:S(2)}) collective-permute-start(f32[528,128]{1,0:T(8,128)S(1)} %get-tuple-element.56), channel_id=1, source_target_pairs={{0,15},{1,2},{2,1},{3,4},{4,3},{5,6},{6,5},{7,8},{8,7},{9,10},{10,... | collective-permute-start | bytes 811016 | tf_op jit(solution)/shard_map/ppermute | solution.py:344
  14.3 40.2 %collective-permute-start.2 = (f32[256,128]{1,0:T(8,128)S(1)}, f32[256,128]{1,0:T(8,128)S(1)}, u32[]{:S(2)}, u32[]{:S(2)}) collective-permute-start(f32[256,128]{1,0:T(8,128)S(1)} %get-tuple-element.53.first_ref), channel_id=1, source_target_pairs={{0,16},{16,32},{32,48},{48,64},{64,80},{80,96},{96,112},{112,128},... | collective-permute-start | bytes 393224 | tf_op jit(solution)/shard_map/ppermute | solution.py:365
  16.2 38.3 %collective-permute-start.3 = (bf16[272,128]{1,0:T(8,128)(2,1)S(1)}, bf16[272,128]{1,0:T(8,128)(2,1)S(1)}, u32[]{:S(2)}, u32[]{:S(2)}) collective-permute-start(bf16[272,128]{1,0:T(8,128)(2,1)S(1)} %get-tuple-element.54), channel_id=1, source_target_pairs={{0,496},{16,32},{32,16},{48,64},{64,48},{80,96},{96,80},{112,128},... | collective-permute-start | bytes 208904 | tf_op jit(solution)/shard_map/ppermute | solution.py:343
  32.5 22.0 %collective-permute-start.4 = (bf16[272,128]{1,0:T(8,128)(2,1)S(1)}, bf16[272,128]{1,0:T(8,128)(2,1)S(1)}, u32[]{:S(2)}, u32[]{:S(2)}) collective-permute-start(bf16[272,128]{1,0:T(8,128)(2,1)S(1)} %get-tuple-element.55), channel_id=1, source_target_pairs={{0,16},{16,0},{32,48},{48,32},{64,80},{80,64},{96,112},{112,96},{1... | collective-permute-start | bytes 208904 | tf_op jit(solution)/shard_map/ppermute | solution.py:345
  34.4 1.0 copy-start.2
  37.8 21.8 %collective-permute-start.1 = (bf16[256,256]{1,0:T(8,128)(2,1)S(1)}, bf16[256,256]{1,0:T(8,128)(2,1)S(1)}, u32[]{:S(2)}, u32[]{:S(2)}) collective-permute-start(bf16[256,256]{1,0:T(8,128)(2,1)S(1)} %get-tuple-element.51), channel_id=1, source_target_pairs={{0,256},{256,0},{1,257},{257,1},{2,258},{258,2},{3,259},{259,3},{4... | collective-permute-start | bytes 393224 | tf_op jit(solution)/shard_map/ppermute | solution.py:371
  48.5 1.0 copy-start.3
  49.6 10.0 %copy-start.13 = (bf16[256,512]{1,0:T(8,128)(2,1)S(1)}, bf16[256,512]{1,0:T(8,128)(2,1)}, u32[]{:S(2)}) copy-start(bf16[256,512]{1,0:T(8,128)(2,1)} %kept_ref.1) | copy-start | bytes 786436
  54.5 44.3 %copy-start = (bf16[1,1,1024,1024]{3,2,1,0:T(8,128)(2,1)S(1)}, bf16[1,1,1024,1024]{3,2,1,0:T(8,128)(2,1)}, u32[]{:S(2)}) copy-start(bf16[1,1,1024,1024]{3,2,1,0:T(8,128)(2,1)} %param.7) | copy-start | bytes 6291460
  59.6 40.6 %copy-start.10 = (f32[1024,128]{1,0:T(8,128)}, f32[1024,128]{1,0:T(8,128)S(1)}, u32[]{:S(2)}) copy-start(f32[1024,128]{1,0:T(8,128)S(1)} %get-tuple-element.62.residual_ref.last_ref) | copy-start | bytes 1572868
  59.6 60.0 %copy-start.5 = (f32[2,256,256]{2,1,0:T(8,128)}, f32[2,256,256]{2,1,0:T(8,128)S(1)}, u32[]{:S(2)}) copy-start(f32[2,256,256]{2,1,0:T(8,128)S(1)} %get-tuple-element.70.refs_8_.slab_factors.refs_10_) | copy-start | bytes 1572868
  89.1 30.5 %copy-start.4 = (bf16[1,1,4,256,256]{4,3,2,1,0:T(8,128)(2,1)S(1)}, bf16[1,1,4,256,256]{4,3,2,1,0:T(8,128)(2,1)}, u32[]{:S(2)}) copy-start(bf16[1,1,4,256,256]{4,3,2,1,0:T(8,128)(2,1)} %param.6) | copy-start | bytes 1572868
  100.2 19.4 %collective-permute-start.6 = (f32[256,128]{1,0:T(8,128)S(1)}, f32[256,128]{1,0:T(8,128)S(1)}, u32[]{:S(2)}, u32[]{:S(2)}) collective-permute-start(f32[256,128]{1,0:T(8,128)S(1)} %get-tuple-element.66), channel_id=1, source_target_pairs={{0,496},{16,32},{32,16},{48,64},{64,48},{80,96},{96,80},{112,128},... | collective-permute-start | bytes 393224 | tf_op jit(solution)/shard_map/ppermute | solution.py:343
  104.3 15.3 %collective-permute-start.7 = (f32[256,128]{1,0:T(8,128)S(1)}, f32[256,128]{1,0:T(8,128)S(1)}, u32[]{:S(2)}, u32[]{:S(2)}) collective-permute-start(f32[256,128]{1,0:T(8,128)S(1)} %get-tuple-element.67), channel_id=1, source_target_pairs={{0,15},{1,2},{2,1},{3,4},{4,3},{5,6},{6,5},{7,8},{8,7},{9,10},{10,... | collective-permute-start | bytes 393224 | tf_op jit(solution)/shard_map/ppermute | solution.py:344
  109.3 10.2 %collective-permute-start.8 = (f32[256,128]{1,0:T(8,128)S(1)}, f32[256,128]{1,0:T(8,128)S(1)}, u32[]{:S(2)}, u32[]{:S(2)}) collective-permute-start(f32[256,128]{1,0:T(8,128)S(1)} %get-tuple-element.68), channel_id=1, source_target_pairs={{0,16},{16,0},{32,48},{48,32},{64,80},{80,64},{96,112},{112,96},{1... | collective-permute-start | bytes 393224 | tf_op jit(solution)/shard_map/ppermute | solution.py:345
  111.3 8.3 %collective-permute-start.9 = (f32[256,128]{1,0:T(8,128)S(1)}, f32[256,128]{1,0:T(8,128)S(1)}, u32[]{:S(2)}, u32[]{:S(2)}) collective-permute-start(f32[256,128]{1,0:T(8,128)S(1)} %get-tuple-element.69), channel_id=1, source_target_pairs={{0,1},{1,0},{2,3},{3,2},{4,5},{5,4},{6,7},{7,6},{8,9},{9,8},{10,11... | collective-permute-start | bytes 393224 | tf_op jit(solution)/shard_map/ppermute | solution.py:346
  126.7 34.1 %all-to-all-start.2 = ((f32[32,2,128]{2,1,0:T(2,128)}), f32[32,2,128]{2,1,0:T(2,128)S(1)}, u32[]{:S(2)}, u32[]{:S(2)}) async-start(f32[32,2,128]{2,1,0:T(2,128)} %get-tuple-element.72), calls=%async_computation.2 | async-start | bytes 65536 | tf_op jit(solution)/shard_map/all_to_all | solution.py:351
  140.5 26.5 %collective-permute-start.10 = (f32[256,128]{1,0:T(8,128)}, f32[256,128]{1,0:T(8,128)}, u32[]{:S(2)}, u32[]{:S(2)}) collective-permute-start(f32[256,128]{1,0:T(8,128)} %copy-done.21), channel_id=1, source_target_pairs={{0,496},{16,32},{32,16},{48,64},{64,48},{80,96},{96,80},{112,128},... | collective-permute-start | bytes 393224 | tf_op jit(solution)/shard_map/ppermute | solution.py:343
  154.3 15.6 %collective-permute-start.11 = (f32[256,128]{1,0:T(8,128)}, f32[256,128]{1,0:T(8,128)}, u32[]{:S(2)}, u32[]{:S(2)}) collective-permute-start(f32[256,128]{1,0:T(8,128)} %copy-done.20), channel_id=1, source_target_pairs={{0,15},{1,2},{2,1},{3,4},{4,3},{5,6},{6,5},{7,8},{8,7},{9,10},{10,... | collective-permute-start | bytes 393224 | tf_op jit(solution)/shard_map/ppermute | solution.py:344
  157.0 12.8 %collective-permute-start.12 = (f32[256,128]{1,0:T(8,128)}, f32[256,128]{1,0:T(8,128)}, u32[]{:S(2)}, u32[]{:S(2)}) collective-permute-start(f32[256,128]{1,0:T(8,128)} %copy-done.19), channel_id=1, source_target_pairs={{0,16},{16,0},{32,48},{48,32},{64,80},{80,64},{96,112},{112,96},{1... | collective-permute-start | bytes 393224 | tf_op jit(solution)/shard_map/ppermute | solution.py:345
  158.9 10.9 %collective-permute-start.13 = (f32[256,128]{1,0:T(8,128)}, f32[256,128]{1,0:T(8,128)}, u32[]{:S(2)}, u32[]{:S(2)}) collective-permute-start(f32[256,128]{1,0:T(8,128)} %copy-done.18), channel_id=1, source_target_pairs={{0,1},{1,0},{2,3},{3,2},{4,5},{5,4},{6,7},{7,6},{8,9},{9,8},{10,11... | collective-permute-start | bytes 393224 | tf_op jit(solution)/shard_map/ppermute | solution.py:346
  161.5 12.0 %all-to-all-start.3 = ((f32[16,2,128]{2,1,0:T(2,128)}), f32[16,2,128]{2,1,0:T(2,128)S(1)}, u32[]{:S(2)}, u32[]{:S(2)}) async-start(f32[16,2,128]{2,1,0:T(2,128)} %sum.3), calls=%async_computation.3 | async-start | bytes 32768 | tf_op jit(solution)/shard_map/all_to_all | solution.py:353
  205.9 59.8 %copy-start.7 = (f32[2,256,256]{2,1,0:T(8,128)S(1)}, f32[2,256,256]{2,1,0:T(8,128)}, u32[]{:S(2)}) copy-start(f32[2,256,256]{2,1,0:T(8,128)} %copy-done.5) | copy-start | bytes 1572868
  205.9 59.8 %copy-start.9 = (f32[1024,128]{1,0:T(8,128)S(1)}, f32[1024,128]{1,0:T(8,128)}, u32[]{:S(2)}) copy-start(f32[1024,128]{1,0:T(8,128)} %copy-done.8) | copy-start | bytes 1572868
  217.2 48.5 %collective-permute-start.14 = (f32[256,128]{1,0:T(8,128)S(1)}, f32[256,128]{1,0:T(8,128)S(1)}, u32[]{:S(2)}, u32[]{:S(2)}) collective-permute-start(f32[256,128]{1,0:T(8,128)S(1)} %get-tuple-element.85), channel_id=1, source_target_pairs={{0,496},{16,32},{32,16},{48,64},{64,48},{80,96},{96,80},{112,128},... | collective-permute-start | bytes 393224 | tf_op jit(solution)/shard_map/ppermute | solution.py:343
  221.4 44.3 %collective-permute-start.15 = (f32[256,128]{1,0:T(8,128)S(1)}, f32[256,128]{1,0:T(8,128)S(1)}, u32[]{:S(2)}, u32[]{:S(2)}) collective-permute-start(f32[256,128]{1,0:T(8,128)S(1)} %get-tuple-element.86), channel_id=1, source_target_pairs={{0,15},{1,2},{2,1},{3,4},{4,3},{5,6},{6,5},{7,8},{8,7},{9,10},{10,... | collective-permute-start | bytes 393224 | tf_op jit(solution)/shard_map/ppermute | solution.py:344
  226.5 39.2 %collective-permute-start.16 = (f32[256,128]{1,0:T(8,128)S(1)}, f32[256,128]{1,0:T(8,128)S(1)}, u32[]{:S(2)}, u32[]{:S(2)}) collective-permute-start(f32[256,128]{1,0:T(8,128)S(1)} %get-tuple-element.87), channel_id=1, source_target_pairs={{0,16},{16,0},{32,48},{48,32},{64,80},{80,64},{96,112},{112,96},{1... | collective-permute-start | bytes 393224 | tf_op jit(solution)/shard_map/ppermute | solution.py:345
  228.5 37.2 %collective-permute-start.17 = (f32[256,128]{1,0:T(8,128)S(1)}, f32[256,128]{1,0:T(8,128)S(1)}, u32[]{:S(2)}, u32[]{:S(2)}) collective-permute-start(f32[256,128]{1,0:T(8,128)S(1)} %get-tuple-element.88), channel_id=1, source_target_pairs={{0,1},{1,0},{2,3},{3,2},{4,5},{5,4},{6,7},{7,6},{8,9},{9,8},{10,11... | collective-permute-start | bytes 393224 | tf_op jit(solution)/shard_map/ppermute | solution.py:346
  268.1 40.3 %collective-permute-start.18 = (f32[256,128]{1,0:T(8,128)S(1)}, f32[256,128]{1,0:T(8,128)S(1)}, u32[]{:S(2)}, u32[]{:S(2)}) collective-permute-start(f32[256,128]{1,0:T(8,128)S(1)} %get-tuple-element.92), channel_id=1, source_target_pairs={{0,496},{16,0},{32,16},{48,32},{64,48},{80,64},{96,80},{112,96},{1... | collective-permute-start | bytes 393224 | tf_op jit(solution)/shard_map/ppermute | solution.py:419
  271.7 36.6 %collective-permute-start.19 = (f32[256,128]{1,0:T(8,128)S(1)}, f32[256,128]{1,0:T(8,128)S(1)}, u32[]{:S(2)}, u32[]{:S(2)}) collective-permute-start(f32[256,128]{1,0:T(8,128)S(1)} %get-tuple-element.93), channel_id=1, source_target_pairs={{0,15},{1,0},{2,1},{3,2},{4,3},{5,4},{6,5},{7,6},{8,7},{9,8},{10,9... | collective-permute-start | bytes 393224 | tf_op jit(solution)/shard_map/ppermute | solution.py:420
  (12 other events, 9.9 us)
